TPU v7x, 32 devices: a whole 2x2x4 slice. The times are simulated.
32 devices in a mesh: group: 2 (over x), tm: 2 (over core), space: 8 (over z, y).
Axes of the slice: x: 2, y: 2, z: 4, core: 2. Of those that a mesh axis runs over, the one named last changes fastest.
Arguments:
- start_old: float32 [4, 3, 1024, 1024], P(('group', 'tm'), None, 'space'), parts along dimension 0, may hold values from -3 to 3
- incoming: float32 [6, 512, 512], P('group', 'space'), parts along dimension 0, may hold values from -3 to 3
Outputs:
- new_states: float32 [4, 3, 1024, 1024], P(('group', 'tm'), None, 'space'), parts along dimension 0
There are 2 independent parts, one for each index of `group`. A program takes and returns all parts, laid end to end along the dimension named above; each array names one. Nothing has to cross between parts.
All inputs are finite; a program needn't handle non-finite values.
Results may differ from a plain program's by a relative error of at most 0.0001.
Values sent between devices are 32-bit elements; how exact they have to be, the bound alone decides.
A program may use at most 192 MiB of HBM per device.

v0:
```python
import math

import jax
import jax.numpy as jnp
from jax import lax
from jax.sharding import PartitionSpec as P

NC = 512
RATIO = 2
STEPS = 2


TIME_STEP = 0.25
CORIOLIS = 0.5
GRAVITY = 1.0
MEAN_DEPTH = 1.0
HIGHEST = lax.Precision.HIGHEST


def extended(shard, sides, width):
    for axis, dim in sides:
        size, length = (lax.axis_size(axis), shard.shape[dim])
        up = [(i, (i + 1) % size) for i in range(size)]
        down = [(j, i) for i, j in up]
        last = lax.slice_in_dim(shard, length - width, length, axis=dim)
        first = lax.slice_in_dim(shard, 0, width, axis=dim)
        before = lax.ppermute(last, axis, up)
        after = lax.ppermute(first, axis, down)
        shard = jnp.concatenate([before, shard, after], axis=dim)
    return shard


def passed_along(block, axis, distance):
    devices = range(lax.axis_size(axis))
    route = [(i - distance, i) for i in devices if i - distance in devices]
    return lax.ppermute(block, axis, route)


def slope_east(field):
    return 0.5 * (jnp.roll(field, -1, -1) - jnp.roll(field, 1, -1))


def slope_north(field):
    return 0.5 * (field[2:] - field[:-2])


def tendency_rows(widened):
    column_depth = MEAN_DEPTH + widened[0]
    flux_east = column_depth * widened[1]
    flux_north = column_depth * widened[2]
    height = widened[0, 1:-1]
    wind_east = widened[1, 1:-1]
    wind_north = widened[2, 1:-1]
    rate_height = -(slope_east(flux_east[1:-1]) + slope_north(flux_north))
    rate_east = (
        -(wind_east * slope_east(wind_east) + wind_north * slope_north(widened[1]))
        + CORIOLIS * wind_north
        - GRAVITY * slope_east(height)
    )
    rate_north = (
        -(wind_east * slope_east(wind_north) + wind_north * slope_north(widened[2]))
        - CORIOLIS * wind_east
        - GRAVITY * slope_north(widened[0])
    )
    return jnp.stack([rate_height, rate_east, rate_north])


def rim_tendency(state):
    widened = extended(state, (("space", 1),), 1)
    return tendency_rows(widened)


def restrict(field):
    fields, rows, cols = field.shape
    return field.reshape(fields, rows // RATIO, RATIO, cols // RATIO, RATIO).mean(axis=(2, 4))


def prolong(field):
    return jnp.repeat(jnp.repeat(field, RATIO, axis=-2), RATIO, axis=-1)


def wavenumbers(count, offset):
    index = offset + jnp.arange(count, dtype=jnp.int32)
    half = NC // 2
    shifted = jnp.where(index < half, index, index - NC)
    shifted = jnp.where(index == half, 0, shifted)
    return shifted.astype(jnp.float32) * (2.0 * math.pi / (NC * RATIO))


def apply_operator(real_part, imag_part, wave_east, wave_north):
    mixed_real = wave_east * real_part[1] + wave_north * real_part[2]
    mixed_imag = wave_east * imag_part[1] + wave_north * imag_part[2]
    height_real = MEAN_DEPTH * mixed_imag
    height_imag = -MEAN_DEPTH * mixed_real
    east_real = GRAVITY * wave_east * imag_part[0] + CORIOLIS * real_part[2]
    east_imag = -GRAVITY * wave_east * real_part[0] + CORIOLIS * imag_part[2]
    north_real = GRAVITY * wave_north * imag_part[0] - CORIOLIS * real_part[1]
    north_imag = -GRAVITY * wave_north * real_part[0] - CORIOLIS * imag_part[1]
    return (
        jnp.stack([height_real, east_real, north_real]),
        jnp.stack([height_imag, east_imag, north_imag]),
    )


def propagate(spectra, wave_east, wave_north, slices):
    duration = slices * (STEPS * TIME_STEP)
    omega = jnp.sqrt(
        CORIOLIS * CORIOLIS
        + GRAVITY * MEAN_DEPTH * (wave_east * wave_east + wave_north * wave_north)
    )
    sine_term = jnp.sin(omega * duration) / omega
    versine_term = (1.0 - jnp.cos(omega * duration)) / (omega * omega)
    once_real, once_imag = apply_operator(spectra[0], spectra[1], wave_east, wave_north)
    twice_real, twice_imag = apply_operator(once_real, once_imag, wave_east, wave_north)
    return jnp.stack(
        [
            spectra[0] + sine_term * once_real + versine_term * twice_real,
            spectra[1] + sine_term * once_imag + versine_term * twice_imag,
        ]
    )


def dft_tables(length):
    index = jnp.arange(length, dtype=jnp.int32)
    phase = index[:, None] * index[None, :] % length
    angle = phase.astype(jnp.float32) * (2.0 * math.pi / length)
    return (jnp.cos(angle), jnp.sin(angle))


def shards(start_old, incoming):
    cosine, sine = dft_tables(NC)
    first_slice = (lax.axis_index("tm") == 0).astype(jnp.float32)
    column_count = NC // lax.axis_size("space")
    wave_east = wavenumbers(column_count, lax.axis_index("space") * column_count)[None, :]
    wave_north = wavenumbers(NC, 0)[:, None]
    start_state = start_old[0]
    drift = restrict(start_state) - first_slice * incoming
    state = start_state
    for step_index in range(STEPS):
        first = state + TIME_STEP * rim_tendency(state)
        state = 0.5 * (state + first + TIME_STEP * rim_tendency(first))
    coarse_fine = restrict(state)
    both_fields = jnp.concatenate([coarse_fine, drift], axis=0)
    real_part = jnp.einsum(
        "fyx,xk->fyk", both_fields, cosine, precision=HIGHEST, preferred_element_type=jnp.float32
    )
    imag_part = -jnp.einsum(
        "fyx,xk->fyk", both_fields, sine, precision=HIGHEST, preferred_element_type=jnp.float32
    )
    piece = lax.all_to_all(
        jnp.stack([real_part, imag_part]), "space", split_axis=3, concat_axis=2, tiled=True
    )
    along_real_part = jnp.einsum(
        "qy,fyk->fqk", cosine, piece[0], precision=HIGHEST, preferred_element_type=jnp.float32
    ) + jnp.einsum(
        "qy,fyk->fqk", sine, piece[1], precision=HIGHEST, preferred_element_type=jnp.float32
    )
    along_imag_part = jnp.einsum(
        "qy,fyk->fqk", cosine, piece[1], precision=HIGHEST, preferred_element_type=jnp.float32
    ) - jnp.einsum(
        "qy,fyk->fqk", sine, piece[0], precision=HIGHEST, preferred_element_type=jnp.float32
    )
    both_spectra = jnp.stack([along_real_part, along_imag_part])
    fine_spectra = both_spectra[:, :3]
    drift_spectra = both_spectra[:, 3:]
    forcing = fine_spectra - propagate(drift_spectra, wave_east, wave_north, 1.0)

    def relay(turn, current):
        previous = passed_along(current, "tm", 1)
        return propagate(previous, wave_east, wave_north, 1.0) + forcing

    carried = lax.fori_loop(0, lax.axis_size("tm") - 1, relay, forcing)
    real_part = jnp.einsum(
        "yq,fqk->fyk", cosine, carried[0], precision=HIGHEST, preferred_element_type=jnp.float32
    ) - jnp.einsum(
        "yq,fqk->fyk", sine, carried[1], precision=HIGHEST, preferred_element_type=jnp.float32
    )
    imag_part = jnp.einsum(
        "yq,fqk->fyk", cosine, carried[1], precision=HIGHEST, preferred_element_type=jnp.float32
    ) + jnp.einsum(
        "yq,fqk->fyk", sine, carried[0], precision=HIGHEST, preferred_element_type=jnp.float32
    )
    piece = lax.all_to_all(
        jnp.stack([real_part, imag_part]), "space", split_axis=2, concat_axis=3, tiled=True
    )
    total = jnp.einsum(
        "fyk,kx->fyx", piece[0], cosine, precision=HIGHEST, preferred_element_type=jnp.float32
    ) - jnp.einsum(
        "fyk,kx->fyx", piece[1], sine, precision=HIGHEST, preferred_element_type=jnp.float32
    )
    coarse_new = total * (1.0 / (NC * NC))
    result = state + prolong(coarse_new - coarse_fine)
    return result[None]


def solution(mesh):
    placed = (P(("group", "tm"), None, "space", None), P("group", "space", None))
    return jax.shard_map(
        shards,
        mesh=mesh,
        in_specs=placed,
        out_specs=P(("group", "tm"), None, "space", None),
        check_vma=False,
    )
```

profile of v0, /device:TPU:0, one launch (start us, length us, event | category | flops | bytes accessed | tf_op | source)
XLA Modules:
  0.0 1148.3 jit_solution(6750687243485078896)
XLA Ops:
  11.9 102.6 %squeeze.67 = f32[3,64,2,512,2]{4,3,2,1,0:T(8,128)} reshape(f32[1,3,128,1024]{3,2,1,0:T(8,128)} %param.2) | data formatting | bytes 3145728 | tf_op jit(solution)/shard_map/squeeze | solution.py:136
  117.1 30.8 %reduce_sum.19 = f32[3,64,512]{2,1,0:T(8,128)S(1)} reduce(f32[3,64,2,512,2]{4,3,2,1,0:T(8,128)} %squeeze.67, f32[]{:T(128)} %constant.27.clone.1), dimensions={2,4}, to_apply=%region_1.2 | reduce | flops 294912 | bytes 1966084 | tf_op jit(solution)/shard_map/reduce_sum | solution.py:75
  148.9 58.0 %copy.254 = f32[3,64,2,512,2]{3,1,4,2,0:T(8,128)} copy(f32[3,64,2,512,2]{4,3,2,1,0:T(8,128)} %squeeze.67) | data formatting | bytes 3145728 | tf_op jit(solution)/shard_map/squeeze | solution.py:136
  233.4 35.6 %reshape.2531 = f32[1,64,2,512,2]{2,1,4,3,0:T(8,128)} reshape(f32[1,128,1024]{1,2,0:T(8,128)} %copy-done.16) | data formatting | bytes 1048576 | tf_op jit(solution)/shard_map/stack | solution.py:65
  269.0 35.7 %reshape.2530 = f32[1,64,2,512,2]{2,1,4,3,0:T(8,128)} reshape(f32[1,128,1024]{1,2,0:T(8,128)} %copy-done.12) | data formatting | bytes 1048576 | tf_op jit(solution)/shard_map/stack | solution.py:65
  304.6 35.6 %reshape.2529 = f32[1,64,2,512,2]{2,1,4,3,0:T(8,128)} reshape(f32[128,1024]{0,1:T(8,128)} %copy-done.8) | data formatting | bytes 1048576 | tf_op jit(solution)/shard_map/stack | solution.py:65
  340.2 20.2 %copy.252 = f32[1,64,2,512,2]{3,1,4,2,0:T(8,128)} copy(f32[1,64,2,512,2]{2,1,4,3,0:T(8,128)} %reshape.2531) | data formatting | bytes 1048576 | tf_op jit(solution)/shard_map/stack | solution.py:65
  360.4 20.2 %copy.251 = f32[1,64,2,512,2]{3,1,4,2,0:T(8,128)} copy(f32[1,64,2,512,2]{2,1,4,3,0:T(8,128)} %reshape.2530) | data formatting | bytes 1048576 | tf_op jit(solution)/shard_map/stack | solution.py:65
  380.7 20.2 %copy.250 = f32[1,64,2,512,2]{3,1,4,2,0:T(8,128)} copy(f32[1,64,2,512,2]{2,1,4,3,0:T(8,128)} %reshape.2529) | data formatting | bytes 1048576 | tf_op jit(solution)/shard_map/stack | solution.py:65
  429.3 35.6 %reshape.2534 = f32[1,64,2,512,2]{2,1,4,3,0:T(8,128)} reshape(f32[1,128,1024]{1,2,0:T(8,128)} %copy-done.26) | data formatting | bytes 1048576 | tf_op jit(solution)/shard_map/stack | solution.py:65
  464.9 35.7 %reshape.2533 = f32[1,64,2,512,2]{2,1,4,3,0:T(8,128)} reshape(f32[1,128,1024]{1,2,0:T(8,128)} %copy-done.20) | data formatting | bytes 1048576 | tf_op jit(solution)/shard_map/stack | solution.py:65
  500.6 35.6 %reshape.2532 = f32[1,64,2,512,2]{2,1,4,3,0:T(8,128)} reshape(f32[128,1024]{0,1:T(8,128)} %copy-done.23) | data formatting | bytes 1048576 | tf_op jit(solution)/shard_map/stack | solution.py:65
  536.1 20.2 %copy.260 = f32[1,64,2,512,2]{3,1,4,2,0:T(8,128)} copy(f32[1,64,2,512,2]{2,1,4,3,0:T(8,128)} %reshape.2534) | data formatting | bytes 1048576 | tf_op jit(solution)/shard_map/stack | solution.py:65
  556.4 20.2 %copy.259 = f32[1,64,2,512,2]{3,1,4,2,0:T(8,128)} copy(f32[1,64,2,512,2]{2,1,4,3,0:T(8,128)} %reshape.2533) | data formatting | bytes 1048576 | tf_op jit(solution)/shard_map/stack | solution.py:65
  576.6 20.2 %copy.258 = f32[1,64,2,512,2]{3,1,4,2,0:T(8,128)} copy(f32[1,64,2,512,2]{2,1,4,3,0:T(8,128)} %reshape.2532) | data formatting | bytes 1048576 | tf_op jit(solution)/shard_map/stack | solution.py:65
  621.6 34.8 %reshape.2537 = f32[1,64,2,512,2]{2,1,4,3,0:T(8,128)} reshape(f32[1,128,1024]{1,2,0:T(8,128)S(1)} %copy-done.35) | data formatting | bytes 1048576 | tf_op jit(solution)/shard_map/stack | solution.py:65
  656.4 34.9 %reshape.2536 = f32[1,64,2,512,2]{2,1,4,3,0:T(8,128)} reshape(f32[1,128,1024]{1,2,0:T(8,128)S(1)} %copy-done.30) | data formatting | bytes 1048576 | tf_op jit(solution)/shard_map/stack | solution.py:65
  691.3 34.8 %reshape.2535 = f32[1,64,2,512,2]{2,1,4,3,0:T(8,128)} reshape(f32[128,1024]{0,1:T(8,128)S(1)} %copy-done.33) | data formatting | bytes 1048576 | tf_op jit(solution)/shard_map/stack | solution.py:65
  726.1 20.2 %copy.266 = f32[1,64,2,512,2]{3,1,4,2,0:T(8,128)} copy(f32[1,64,2,512,2]{2,1,4,3,0:T(8,128)} %reshape.2537) | data formatting | bytes 1048576 | tf_op jit(solution)/shard_map/stack | solution.py:65
  746.4 20.2 %copy.265 = f32[1,64,2,512,2]{3,1,4,2,0:T(8,128)} copy(f32[1,64,2,512,2]{2,1,4,3,0:T(8,128)} %reshape.2536) | data formatting | bytes 1048576 | tf_op jit(solution)/shard_map/stack | solution.py:65
  766.6 20.2 %copy.264 = f32[1,64,2,512,2]{3,1,4,2,0:T(8,128)} copy(f32[1,64,2,512,2]{2,1,4,3,0:T(8,128)} %reshape.2535) | data formatting | bytes 1048576 | tf_op jit(solution)/shard_map/stack | solution.py:65
  798.9 35.6 %reshape.2540 = f32[1,64,2,512,2]{2,1,4,3,0:T(8,128)} reshape(f32[1,128,1024]{1,2,0:T(8,128)} %fusion.51) | data formatting | bytes 1048576 | tf_op jit(solution)/shard_map/stack | solution.py:65
  834.5 20.3 %copy.272 = f32[1,64,2,512,2]{3,1,4,2,0:T(8,128)} copy(f32[1,64,2,512,2]{2,1,4,3,0:T(8,128)} %reshape.2540) | data formatting | bytes 1048576 | tf_op jit(solution)/shard_map/stack | solution.py:65
  854.7 34.8 %reshape.2539 = f32[1,64,2,512,2]{2,1,4,3,0:T(8,128)} reshape(f32[1,128,1024]{1,2,0:T(8,128)S(1)} %copy-done.38) | data formatting | bytes 1048576 | tf_op jit(solution)/shard_map/stack | solution.py:65
  889.5 20.4 %copy.271 = f32[1,64,2,512,2]{3,1,4,2,0:T(8,128)} copy(f32[1,64,2,512,2]{2,1,4,3,0:T(8,128)} %reshape.2539) | data formatting | bytes 1048576 | tf_op jit(solution)/shard_map/stack | solution.py:65
  910.9 34.8 %reshape.2538 = f32[1,64,2,512,2]{2,1,4,3,0:T(8,128)} reshape(f32[128,1024]{0,1:T(8,128)S(1)} %fusion.66) | data formatting | bytes 1048576 | tf_op jit(solution)/shard_map/stack | solution.py:65
  945.7 20.4 %copy.270 = f32[1,64,2,512,2]{3,1,4,2,0:T(8,128)} copy(f32[1,64,2,512,2]{2,1,4,3,0:T(8,128)} %reshape.2538) | data formatting | bytes 1048576 | tf_op jit(solution)/shard_map/stack | solution.py:65
  995.0 33.9 %all-to-all-done = f32[8,1,49152]{2,1,0:T(1,128)S(1)} async-done(((f32[8,1,49152]{2,1,0:T(1,128)}), f32[8,1,49152]{2,1,0:T(1,128)S(1)}, u32[]{:S(2)}, u32[]{:S(2)}) %all-to-all-start) | async-done | bytes 1572896 | tf_op jit(solution)/shard_map/all_to_all | solution.py:150
  1029.3 6.1 reduce
  1042.4 6.8 fusion.40
  1061.3 5.8 fusion.14
  1095.9 24.7 %all_to_all.30 = f32[8,1,24576]{2,1,0:T(1,128)S(1)} all-to-all(f32[8,1,24576]{2,1,0:T(1,128)S(1)} %reshape.2543), channel_id=1, replica_groups=mesh['group'=2,'tm'=2,'space'=8] {'space'}, dimensions={0} | all-to-all | bytes 1572864 | tf_op jit(solution)/shard_map/all_to_all | solution.py:183
  (265 shorter events, 211.6 us)
Async XLA Ops:
  1.9 605.5 %copy-start = (f32[1,3,128,1024]{2,3,1,0:T(8,128)}, f32[1,3,128,1024]{2,3,1,0:T(8,128)S(1)}, u32[]{:S(2)}) copy-start(f32[1,3,128,1024]{2,3,1,0:T(8,128)S(1)} %copy.228) | copy-start | bytes 4718596
  5.4 201.5 %collective-permute-start = (f32[3,1,1024]{2,1,0:T(1,128)S(1)}, f32[3,1,1024]{2,1,0:T(1,128)S(1)}, u32[]{:S(2)}, u32[]{:S(2)}) collective-permute-start(f32[3,1,1024]{2,1,0:T(1,128)S(1)} %copy.218), channel_id=1, source_target_pairs={{0,1},{1,2},{2,3},{3,4},{4,5},{5,6},{6,7},{7,0},{8,9},{9,10},{10,1... | collective-permute-start | bytes 36872 | tf_op jit(solution)/shard_map/ppermute | solution.py:27
  8.9 198.5 %collective-permute-start.1 = (f32[3,1,1024]{2,1,0:T(1,128)S(1)}, f32[3,1,1024]{2,1,0:T(1,128)S(1)}, u32[]{:S(2)}, u32[]{:S(2)}) collective-permute-start(f32[3,1,1024]{2,1,0:T(1,128)S(1)} %copy.219), channel_id=1, source_target_pairs={{1,0},{2,1},{3,2},{4,3},{5,4},{6,5},{7,6},{0,7},{9,8},{10,9},{11,1... | collective-permute-start | bytes 36872 | tf_op jit(solution)/shard_map/ppermute | solution.py:28
  117.1 30.9 %copy-start.55 = (f32[3,64,512]{2,1,0:T(8,128)S(1)}, f32[3,64,512]{2,1,0:T(8,128)}, u32[]{:S(2)}) copy-start(f32[3,64,512]{2,1,0:T(8,128)} %param.3) | copy-start | bytes 1179652
  223.6 177.3 %collective-permute-start.2 = (f32[3,1,1024]{2,1,0:T(1,128)S(1)}, f32[3,1,1024]{2,1,0:T(1,128)S(1)}, u32[]{:S(2)}, u32[]{:S(2)}) collective-permute-start(f32[3,1,1024]{2,1,0:T(1,128)S(1)} %copy.229), channel_id=1, source_target_pairs={{0,1},{1,2},{2,3},{3,4},{4,5},{5,6},{6,7},{7,0},{8,9},{9,10},{10,1... | collective-permute-start | bytes 36872 | tf_op jit(solution)/shard_map/ppermute | solution.py:27
  225.5 177.1 %collective-permute-start.3 = (f32[3,1,1024]{2,1,0:T(1,128)S(1)}, f32[3,1,1024]{2,1,0:T(1,128)S(1)}, u32[]{:S(2)}, u32[]{:S(2)}) collective-permute-start(f32[3,1,1024]{2,1,0:T(1,128)S(1)} %copy.230), channel_id=1, source_target_pairs={{1,0},{2,1},{3,2},{4,3},{5,4},{6,5},{7,6},{0,7},{9,8},{10,9},{11,1... | collective-permute-start | bytes 36872 | tf_op jit(solution)/shard_map/ppermute | solution.py:28
  406.7 4.8 copy-start.20
  419.2 177.6 %collective-permute-start.4 = (f32[3,1,1024]{2,1,0:T(1,128)S(1)}, f32[3,1,1024]{2,1,0:T(1,128)S(1)}, u32[]{:S(2)}, u32[]{:S(2)}) collective-permute-start(f32[3,1,1024]{2,1,0:T(1,128)S(1)} %copy.235), channel_id=1, source_target_pairs={{0,1},{1,2},{2,3},{3,4},{4,5},{5,6},{6,7},{7,0},{8,9},{9,10},{10,1... | collective-permute-start | bytes 36872 | tf_op jit(solution)/shard_map/ppermute | solution.py:27
  421.1 177.4 %collective-permute-start.5 = (f32[3,1,1024]{2,1,0:T(1,128)S(1)}, f32[3,1,1024]{2,1,0:T(1,128)S(1)}, u32[]{:S(2)}, u32[]{:S(2)}) collective-permute-start(f32[3,1,1024]{2,1,0:T(1,128)S(1)} %copy.236), channel_id=1, source_target_pairs={{1,0},{2,1},{3,2},{4,3},{5,4},{6,5},{7,6},{0,7},{9,8},{10,9},{11,1... | collective-permute-start | bytes 36872 | tf_op jit(solution)/shard_map/ppermute | solution.py:28
  602.6 4.8 copy-start.29
  613.7 6.9 copy-start.37
  613.7 173.1 %collective-permute-start.6 = (f32[3,1,1024]{2,1,0:T(1,128)S(1)}, f32[3,1,1024]{2,1,0:T(1,128)S(1)}, u32[]{:S(2)}, u32[]{:S(2)}) collective-permute-start(f32[3,1,1024]{2,1,0:T(1,128)S(1)} %copy.241), channel_id=1, source_target_pairs={{0,1},{1,2},{2,3},{3,4},{4,5},{5,6},{6,7},{7,0},{8,9},{9,10},{10,1... | collective-permute-start | bytes 36872 | tf_op jit(solution)/shard_map/ppermute | solution.py:27
  613.7 7.9 copy-start.35
  615.7 171.6 %collective-permute-start.7 = (f32[3,1,1024]{2,1,0:T(1,128)S(1)}, f32[3,1,1024]{2,1,0:T(1,128)S(1)}, u32[]{:S(2)}, u32[]{:S(2)}) collective-permute-start(f32[3,1,1024]{2,1,0:T(1,128)S(1)} %copy.242), channel_id=1, source_target_pairs={{1,0},{2,1},{3,2},{4,3},{5,4},{6,5},{7,6},{0,7},{9,8},{10,9},{11,1... | collective-permute-start | bytes 36872 | tf_op jit(solution)/shard_map/ppermute | solution.py:28
  621.6 34.8 %copy-start.30 = (f32[1,128,1024]{1,2,0:T(8,128)S(1)}, f32[1,128,1024]{1,2,0:T(8,128)}, u32[]{:S(2)}) copy-start(f32[1,128,1024]{1,2,0:T(8,128)} %copy-done.29) | copy-start | bytes 1572868
  656.4 34.9 %copy-start.33 = (f32[128,1024]{0,1:T(8,128)S(1)}, f32[128,1024]{0,1:T(8,128)}, u32[]{:S(2)}) copy-start(f32[128,1024]{0,1:T(8,128)} %copy-done.32) | copy-start | bytes 1572868
  834.4 20.3 %copy-start.38 = (f32[1,128,1024]{1,2,0:T(8,128)S(1)}, f32[1,128,1024]{1,2,0:T(8,128)}, u32[]{:S(2)}) copy-start(f32[1,128,1024]{1,2,0:T(8,128)} %get-tuple-element.55) | copy-start | bytes 1572868
  889.5 20.4 %copy-start.40 = (f32[1,130,1024]{1,2,0:T(8,128)S(1)}, f32[1,130,1024]{1,2,0:T(8,128)}, u32[]{:S(2)}) copy-start(f32[1,130,1024]{1,2,0:T(8,128)} %get-tuple-element.43) | copy-start | bytes 1597444
  889.5 20.4 %copy-start.46 = (f32[128,1023]{0,1:T(8,128)S(1)}, f32[128,1023]{0,1:T(8,128)}, u32[]{:S(2)}) copy-start(f32[128,1023]{0,1:T(8,128)} %get-tuple-element.82) | copy-start | bytes 1571332
  889.5 20.4 %copy-start.47 = (f32[128,1023]{0,1:T(8,128)S(1)}, f32[128,1023]{0,1:T(8,128)}, u32[]{:S(2)}) copy-start(f32[128,1023]{0,1:T(8,128)} %get-tuple-element.83) | copy-start | bytes 1571332
  945.7 20.4 %copy-start.36 = (f32[3,64,2,512,2]{3,1,4,2,0:T(8,128)S(1)}, f32[3,64,2,512,2]{3,1,4,2,0:T(8,128)}, u32[]{:S(2)}) copy-start(f32[3,64,2,512,2]{3,1,4,2,0:T(8,128)} %copy.254) | copy-start | bytes 4718596
  945.7 20.4 %copy-start.41 = (f32[1,64,2,512,2]{3,1,4,2,0:T(8,128)S(1)}, f32[1,64,2,512,2]{3,1,4,2,0:T(8,128)}, u32[]{:S(2)}) copy-start(f32[1,64,2,512,2]{3,1,4,2,0:T(8,128)} %copy.252) | copy-start | bytes 1572868
  945.7 20.4 %copy-start.42 = (f32[1,64,2,512,2]{3,1,4,2,0:T(8,128)S(1)}, f32[1,64,2,512,2]{3,1,4,2,0:T(8,128)}, u32[]{:S(2)}) copy-start(f32[1,64,2,512,2]{3,1,4,2,0:T(8,128)} %copy.251) | copy-start | bytes 1572868
  945.7 20.4 %copy-start.43 = (f32[1,64,2,512,2]{3,1,4,2,0:T(8,128)S(1)}, f32[1,64,2,512,2]{3,1,4,2,0:T(8,128)}, u32[]{:S(2)}) copy-start(f32[1,64,2,512,2]{3,1,4,2,0:T(8,128)} %copy.250) | copy-start | bytes 1572868
  989.8 39.0 %all-to-all-start = ((f32[8,1,49152]{2,1,0:T(1,128)}), f32[8,1,49152]{2,1,0:T(1,128)S(1)}, u32[]{:S(2)}, u32[]{:S(2)}) async-start(f32[8,1,49152]{2,1,0:T(1,128)} %reshape.2541), calls=%async_computation | async-start | bytes 3145728 | tf_op jit(solution)/shard_map/all_to_all | solution.py:150
  1055.4 5.9 copy-start.54
  1068.6 3.2 collective-permute-start.8
  1135.9 5.9 copy-start.15
  1135.9 5.9 copy-start.19
  1135.9 5.9 copy-start.22
  1135.9 5.9 copy-start.25
  1135.9 5.9 copy-start.28
  (35 other events, 63.0 us)
where the time goes:
time: 1160 us; the launch traced here: 1150 us
  local copies, waits for them, and re-layouts  921 us (79%)
  other arithmetic  74.1 us (6%)
  matrix products  65.3 us (6%)
  waiting for transfers between devices  35.6 us (3%)
  starting transfers between devices  26.4 us (2%)
  blocking collectives  24.7 us (2%)
    another operation x24, local copies, waits for them, and re-layouts, tendency_rows(): return jnp.stack([rate_height, rate_east, rate_north])  666 us
    squeeze x2, local copies, waits for them, and re-layouts, shards(): start_state = start_old[0]  161 us
    reduce_sum x2, other arithmetic, restrict(): field.reshape(fields, rows // RATIO, RATIO, cols // RATIO, RATIO)  34.1 us
    all_to_all x1, waiting for transfers between devices, shards(): lax.all_to_all(jnp.stack([real_part, imag_part]), 'space', split_axis=3,...  33.9 us
    unnamed x119, local copies, waits for them, and re-layouts  24.8 us
    all_to_all x1, blocking collectives, shards(): lax.all_to_all(jnp.stack([real_part, imag_part]), 'space', split_axis=2,...  24.7 us
  transfers between devices with their start and end apart: 10, of which 2 were waited for; matrix products, arithmetic and copies ran while one was open for 62% of the time, Pallas kernels for 0%

commit v1 on v0

v1 whole, which is shorter than its diff:
```python
import math

import jax
import jax.numpy as jnp
import numpy as np
from jax import lax
from jax.experimental import pallas as pl
from jax.experimental.pallas import tpu as pltpu
from jax.sharding import PartitionSpec as P

RATIO = 2
STEPS = 2
TIME_STEP = 0.25
CORIOLIS = 0.5
HALO = 8
HIGH = lax.Precision.HIGH


def dot(spec, a, b):
    return jnp.einsum(spec, a, b, precision=HIGH, preferred_element_type=jnp.float32)


def tables(nc, parts):
    half, rows = nc // 2, nc // parts
    x = np.arange(nc)
    angle = 2.0 * math.pi / nc * (np.outer(np.arange(half), x) % nc)
    real, imag = np.cos(angle), -np.sin(angle)
    imag[0] = (-1.0) ** x
    forward = np.stack([real, imag])
    wide = 0.5 * np.repeat(forward, RATIO, axis=2)

    angle = 2.0 * math.pi / nc * (np.outer(x, x) % nc)
    cos, sin = np.cos(angle), np.sin(angle)
    along = np.stack([np.stack([cos, -sin], 1), np.stack([sin, cos], 1)])
    back = np.stack([np.stack([cos, sin], 1), np.stack([-sin, cos], 1)])
    along = along.reshape(2, parts, rows, 2 * nc).transpose(1, 0, 2, 3).reshape(2 * nc, 2 * nc)
    back = back.reshape(2 * nc, 2, parts, rows).transpose(0, 2, 1, 3).reshape(2 * nc, 2 * nc)

    scale = np.full((1, half, 1), 2.0 / (nc * nc))
    scale[:, 0] = 1.0 / (nc * nc)
    inverse = np.repeat(forward * scale, RATIO, axis=2)

    index = np.where(x < half, x, x - nc)
    index = np.where(x == half, 0, index)
    wave = index * (2.0 * math.pi / (nc * RATIO))
    omega = np.sqrt(CORIOLIS**2 + wave[:half, None] ** 2 + wave[None, :] ** 2)
    duration = STEPS * TIME_STEP
    sine = np.sin(omega * duration) / omega
    versine = (1.0 - np.cos(omega * duration)) / omega**2
    single = lambda a: np.asarray(a, np.float32)
    return [single(a) for a in (forward, wide, along, back, inverse, wave, sine, versine)]


def tendency(window):
    width = window[0].shape[-1]
    mid = [a[8:16] for a in window]
    south = [a[7:15] for a in window]
    north = [a[9:17] for a in window]
    west = [pltpu.roll(a, 1, 1) for a in mid]
    east = [pltpu.roll(a, width - 1, 1) for a in mid]
    _, u, v = mid
    flux = (1.0 + east[0]) * east[1] - (1.0 + west[0]) * west[1]
    flux = flux + ((1.0 + north[0]) * north[2] - (1.0 + south[0]) * south[2])
    half_u, half_v = 0.5 * u, 0.5 * v
    rate_u = CORIOLIS * v - (
        half_u * (east[1] - west[1]) + half_v * (north[1] - south[1]) + 0.5 * (east[0] - west[0])
    )
    rate_v = -(CORIOLIS * u) - (
        half_u * (east[2] - west[2]) + half_v * (north[2] - south[2]) + 0.5 * (north[0] - south[0])
    )
    return mid, (-0.5 * flux, rate_u, rate_v)


def heun_kernel(before, state, after, fine, now, first):
    rows = state.shape[1]
    blocks = (rows + 2 * HALO) // 8
    for f in range(3):
        now[f, 8:16] = before[f]
        now[f, 16 : 16 + rows] = state[f]
        now[f, 16 + rows : 24 + rows] = after[f]

    def window(ref, block):
        at = pl.multiple_of(block * 8, 8)
        return [ref[f, pl.ds(at, 24)] for f in range(3)]

    def predict(block, _):
        mid, rate = tendency(window(now, block))
        at = pl.multiple_of(block * 8 + 8, 8)
        for f in range(3):
            first[f, pl.ds(at, 8)] = mid[f] + TIME_STEP * rate[f]
        return 0

    def correct(out, shift):
        def body(block, _):
            mid, rate = tendency(window(first, block))
            at = pl.multiple_of(block * 8 + 8, 8)
            to = pl.multiple_of(block * 8 + 8 - shift, 8)
            for f in range(3):
                out[f, pl.ds(to, 8)] = 0.5 * (now[f, pl.ds(at, 8)] + mid[f] + TIME_STEP * rate[f])
            return 0

        return body

    for step in range(STEPS):
        lax.fori_loop(0, blocks, predict, 0)
        if step < STEPS - 1:
            lax.fori_loop(0, blocks, correct(now, 0), 0)
        else:
            lax.fori_loop(1, blocks - 1, correct(fine, 16), 0)


def heun(before, state, after):
    fields, rows, width = state.shape
    vmem = pl.BlockSpec(memory_space=pltpu.VMEM)
    padded = pltpu.VMEM((fields, rows + 4 * HALO, width), jnp.float32)
    return pl.pallas_call(
        heun_kernel,
        out_shape=jax.ShapeDtypeStruct(state.shape, jnp.float32),
        in_specs=[vmem] * 3,
        out_specs=vmem,
        scratch_shapes=[padded, padded],
        compiler_params=pltpu.CompilerParams(vmem_limit_bytes=24 << 20),
        cost_estimate=pl.CostEstimate(
            flops=200 * rows * width, bytes_accessed=24 * rows * width, transcendentals=0
        ),
    )(before, state, after)


def apply_operator(s, wave_east, wave_north):
    turn = lambda a: jnp.stack([a[:, 1], -a[:, 0]], 1)
    h, u, v = s
    return (
        turn(wave_east * u + wave_north * v),
        wave_east * turn(h) + CORIOLIS * v,
        wave_north * turn(h) - CORIOLIS * u,
    )


def propagate(s, wave_east, wave_north, sine, versine):
    once = apply_operator(s, wave_east, wave_north)
    twice = apply_operator(once, wave_east, wave_north)
    return jnp.stack([a + sine * b + versine * c for a, b, c in zip(s, once, twice)])


def shards(start_old, incoming):
    size, slices = lax.axis_size("space"), lax.axis_size("tm")
    state = start_old[0]
    _, fine_rows, width = state.shape
    rows, nc = incoming.shape[1:]
    half = nc // 2
    count = half // size
    forward, wide, along, back, inverse, wave, sine, versine = tables(nc, size)
    pairs = np.repeat(np.eye(rows, dtype=np.float32), RATIO, axis=1)

    up = [(i, (i + 1) % size) for i in range(size)]
    down = [(j, i) for i, j in up]
    before = lax.ppermute(state[:, fine_rows - HALO :], "space", up)
    after = lax.ppermute(state[:, :HALO], "space", down)

    is_first = (lax.axis_index("tm") == 0).astype(jnp.float32)
    start_rows = dot("yY,fYx->fyx", 0.5 * pairs, state)
    drift = dot("ckx,fyx->ckfy", wide, start_rows)
    drift = drift - dot("ckx,fyx->ckfy", forward, is_first * incoming)

    fine = heun(before, state, after)
    coarse_rows = dot("yY,fYx->fyx", 0.5 * pairs, fine)
    coarse = dot("ckx,fyx->ckfy", wide, coarse_rows)
    route = [(i, i + 1) for i in range(slices - 1)]
    gap = lax.ppermute(coarse, "tm", route) - drift

    gap = gap.reshape(2, size, count, 3, rows).transpose(1, 3, 2, 0, 4)
    gap = gap.reshape(size, 3 * count, 2 * rows)
    piece = lax.all_to_all(gap, "space", 0, 0)
    spectra = dot("imy,iyq->mq", piece, along.reshape(size, 2 * rows, 2 * nc))
    spectra = spectra.reshape(3, count, 2, nc)

    mine = lax.axis_index("space") * count
    cut = lambda a: lax.dynamic_slice_in_dim(jnp.asarray(a), mine, count, 0)
    wave_east = cut(wave[:half])[:, None, None]
    wave_north = wave[None, None, :]
    factors = (wave_east, wave_north, cut(sine)[:, None, :], cut(versine)[:, None, :])
    change = propagate(spectra, *factors)
    for _ in range(slices - 1):
        change = propagate(spectra + lax.ppermute(change, "tm", route), *factors)

    change = change.reshape(3 * count, 2 * nc)
    moved = dot("mq,qiy->imy", change, back.reshape(2 * nc, size, 2 * rows))
    moved = lax.all_to_all(moved, "space", 0, 0)
    moved = moved.reshape(size, 3, count, 2, rows).transpose(1, 4, 3, 0, 2)
    moved = moved.reshape(3, rows, nc)
    moved = dot("yY,fyk->fYk", pairs, moved)
    result = fine + dot("fYk,kx->fYx", moved, inverse.reshape(nc, width))
    return result[None]


def solution(mesh):
    placed = (P(("group", "tm"), None, "space", None), P("group", "space", None))
    return jax.shard_map(
        shards,
        mesh=mesh,
        in_specs=placed,
        out_specs=P(("group", "tm"), None, "space", None),
        check_vma=False,
    )
```

time: 1160 us -> 82.5 us (0.07)
  local copies, waits for them, and re-layouts: 921 us -> 8.38 us
  other arithmetic: 74.1 us -> 3.59 us
  matrix products: 65.3 us -> 14.6 us
  waiting for transfers between devices: 35.6 us -> 15.1 us
  starting transfers between devices: 26.4 us -> 13.9 us
    another operation x26 -> x8, local copies, waits for them, and re-layouts: 672 us -> 0.7 us  [the longest x4 0.44 us: apply_operator(): h, u, v = s]
    squeeze x10 -> x0, local copies, waits for them, and re-layouts: 165 us -> none  [the longest x2 161 us: shards(): start_state = start_old[0]]
    dot_general x12 -> x9, matrix products: 65.3 us -> 14.6 us  [dot(): jnp.einsum(spec, a, b, precision=HIGH, preferred_element_type=jnp.float32)]
    reduce_sum x2 -> x0, other arithmetic: 34.1 us -> none  [restrict(): field.reshape(fields, rows // RATIO, RATIO, cols // RATIO, RATIO)]
    all_to_all x1, waiting for transfers between devices: 33.9 us -> 10.7 us  [shards(): piece = lax.all_to_all(gap, 'space', 0, 0)]
    unnamed x119 -> x18, local copies, waits for them, and re-layouts: 24.8 us -> 2.46 us
    slice x22 -> x1, local copies, waits for them, and re-layouts: 22.7 us -> 0.96 us  [shards(): after = lax.ppermute(state[:, :HALO], 'space', down)]
    sub x13 -> x0, other arithmetic: 14 us -> none  [the longest x4 8.39 us: tendency_rows(): -(wind_east * slope_east(wind_east) + wind_north * slope_north(widened[1]))]
  transfers between devices with their start and end apart: 10 -> 5, of which waited for: 2 -> 4; matrix products, arithmetic and copies ran while one was open for 62% -> 4% of each run, Pallas kernels for 0% -> 0%
where the time goes in v1:
time: 82.5 us; the launch traced here: 81.9 us
  blocking collectives  16.3 us (20%)
  waiting for transfers between devices  15.1 us (18%)
  matrix products  14.6 us (18%)
  starting transfers between devices  13.9 us (17%)
  Pallas kernels  9.59 us (12%)
  local copies, waits for them, and re-layouts  8.38 us (10%)
  other arithmetic  3.59 us (4%)
    all_to_all x1, blocking collectives, shards(): moved = lax.all_to_all(moved, 'space', 0, 0)  16.3 us
    dot_general x9, matrix products, dot(): jnp.einsum(spec, a, b, precision=HIGH, preferred_element_type=jnp.float32)  14.6 us
    all_to_all x1, waiting for transfers between devices, shards(): piece = lax.all_to_all(gap, 'space', 0, 0)  10.7 us
    pallas_call x1, Pallas kernels, heun(): pl.pallas_call(heun_kernel, out_shape=jax.ShapeDtypeStruct(state.shape, j...  9.59 us
    all_to_all x1, starting transfers between devices, shards(): piece = lax.all_to_all(gap, 'space', 0, 0)  4.96 us
    ppermute x1, starting transfers between devices, shards(): after = lax.ppermute(state[:, :HALO], 'space', down)  3.1 us
    ppermute x1, starting transfers between devices, shards(): before = lax.ppermute(state[:, fine_rows - HALO:], 'space', up)  3.02 us
    ppermute x1, waiting for transfers between devices, shards(): before = lax.ppermute(state[:, fine_rows - HALO:], 'space', up)  2.83 us
  transfers between devices with their start and end apart: 5, of which 4 were waited for; matrix products, arithmetic and copies ran while one was open for 4% of the time, Pallas kernels for 0%

profile of v1, /device:TPU:0, one launch (start us, length us, event | category | flops | bytes accessed | tf_op | source)
XLA Modules:
  0.0 81.9 jit_solution(5006284943509335728)
XLA Ops:
  0.0 1.0 %fusion.22 = (f32[3,8,1024]{2,1,0:T(8,128)S(1)}, f32[3,8,1024]{2,1,0:T(8,128)S(1)}) fusion(f32[3,128,1024]{2,1,0:T(8,128)} %bitcast.109), kind=kLoop, calls=%fused_computation.72 | loop fusion | bytes 393216 | tf_op jit(solution)/shard_map/slice | solution.py:158
  1.0 3.0 %collective-permute-start = (f32[3,8,1024]{2,1,0:T(8,128)S(1)}, f32[3,8,1024]{2,1,0:T(8,128)S(1)}, u32[]{:S(2)}, u32[]{:S(2)}) collective-permute-start(f32[3,8,1024]{2,1,0:T(8,128)S(1)} %get-tuple-element.6), channel_id=1, source_target_pairs={{0,1},{1,2},{2,3},{3,4},{4,5},{5,6},{6,7},{7,0},{8,9},{9,10},{10,1... | collective-permute-start | bytes 294920 | tf_op jit(solution)/shard_map/ppermute | solution.py:157
  4.0 3.1 %collective-permute-start.1 = (f32[3,8,1024]{2,1,0:T(8,128)S(1)}, f32[3,8,1024]{2,1,0:T(8,128)S(1)}, u32[]{:S(2)}, u32[]{:S(2)}) collective-permute-start(f32[3,8,1024]{2,1,0:T(8,128)S(1)} %get-tuple-element.5), channel_id=1, source_target_pairs={{1,0},{2,1},{3,2},{4,3},{5,4},{6,5},{7,6},{0,7},{9,8},{10,9},{11,1... | collective-permute-start | bytes 294920 | tf_op jit(solution)/shard_map/ppermute | solution.py:158
  7.1 2.8 %collective-permute-done.before = f32[3,8,1024]{2,1,0:T(8,128)S(1)} collective-permute-done((f32[3,8,1024]{2,1,0:T(8,128)S(1)}, f32[3,8,1024]{2,1,0:T(8,128)S(1)}, u32[]{:S(2)}, u32[]{:S(2)}) %collective-permute-start) | collective-permute-done | bytes 98336 | tf_op jit(solution)/shard_map/ppermute | solution.py:157
  9.9 0.8 collective-permute-done.1.after
  10.7 1.4 %copy-done = f32[1,3,128,1024]{3,2,1,0:T(8,128)S(1)} copy-done((f32[1,3,128,1024]{3,2,1,0:T(8,128)S(1)}, f32[1,3,128,1024]{3,2,1,0:T(8,128)}, u32[]{:S(2)}) %copy-start) | copy-done | bytes 1572888
  12.1 9.6 %shard_map.145 = f32[3,128,1024]{2,1,0:T(8,128)S(1)} custom-call(f32[3,8,1024]{2,1,0:T(8,128)S(1)} %collective-permute-done.before, f32[3,128,1024]{2,1,0:T(8,128)S(1)} %bitcast.110, f32[3,8,1024]{2,1,0:T(8,128)S(1)} %collective-permute-done.1.after), custom_call_target="tpu_custom_call" | custom-call | flops 26214400 | bytes 3145728 | tf_op jit(solution)/shard_map/pallas_call | solution.py:116
  21.7 0.6 convolution_bitcast_fusion.1
  22.3 1.2 %fusion.26 = f32[2,256,3,64]{1,3,2,0:T(8,128)S(1)} fusion(f32[2,256,1024,1]{2,1,3,0:T(8,128)S(1)} %copy-done.1, f32[3,64,1024,1]{2,1,0,3:T(8,128)S(1)} %convolution_bitcast_fusion.1), kind=kOutput, calls=%fused_computation.76 | convolution fusion | flops 603979776 | bytes 3276800 | tf_op jit(solution)/shard_map/ckx,fyx->ckfy/dot_general | solution.py:20
  23.5 1.3 %collective-permute-start.2 = (f32[2,256,3,64]{1,3,2,0:T(8,128)S(1)}, f32[2,256,3,64]{1,3,2,0:T(8,128)S(1)}, u32[]{:S(2)}, u32[]{:S(2)}) collective-permute-start(f32[2,256,3,64]{1,3,2,0:T(8,128)S(1)} %fusion.26), channel_id=1, source_target_pairs={{0,8},{1,9},{2,10},{3,11},{4,12},{5,13},{6,14},{7,15},{16,24},{17,... | collective-permute-start | bytes 1179656 | tf_op jit(solution)/shard_map/ppermute | solution.py:169
  24.8 0.5 convolution_bitcast_fusion
  25.4 1.2 %fusion.27 = f32[3,64,2,256]{3,1,0,2:T(8,128)S(1)} fusion(f32[3,64,1024,1]{2,1,0,3:T(8,128)S(1)} %convolution_bitcast_fusion, f32[2,256,1024,1]{2,1,3,0:T(8,128)S(1)} %copy-done.1), kind=kOutput, calls=%fused_computation.77 | convolution fusion | flops 603979776 | bytes 3276800 | tf_op jit(solution)/shard_map/ckx,fyx->ckfy/dot_general | solution.py:20
  26.7 0.7 fusion.1
  27.6 0.6 copy.22
  28.3 1.2 %reshape.483 = f32[8,96,128]{2,1,0:T(8,128)} reshape(f32[8,3,32,2,64]{4,3,2,1,0:T(2,128)S(1)} %copy.22) | data formatting | bytes 786432 | tf_op jit(solution)/shard_map/reshape | solution.py:172
  29.5 5.0 %all-to-all-start = ((f32[8,96,128]{2,1,0:T(8,128)}), f32[8,96,128]{2,1,0:T(8,128)S(1)}, u32[]{:S(2)}, u32[]{:S(2)}) async-start(f32[8,96,128]{2,1,0:T(8,128)} %reshape.483), calls=%async_computation | async-start | bytes 786432 | tf_op jit(solution)/shard_map/all_to_all | solution.py:173
  34.5 0.9 %constant_dynamic-slice_fusion = (f32[32,512]{1,0:T(8,128)S(1)}, f32[32,512]{1,0:T(8,128)S(1)}) fusion(f32[256,512]{1,0:T(8,128)} %constant.45.clone, s32[]{:T(128)S(6)} %select_n.2, f32[256,512]{1,0:T(8,128)} %constant.44.clone), kind=kLoop, calls=%fused_computation.65 | loop fusion | bytes 262148 | tf_op jit(solution)/shard_map/dynamic_slice | solution.py:178
  35.4 10.7 %all-to-all-done = f32[8,96,128]{2,1,0:T(8,128)S(1)} async-done(((f32[8,96,128]{2,1,0:T(8,128)}), f32[8,96,128]{2,1,0:T(8,128)S(1)}, u32[]{:S(2)}, u32[]{:S(2)}) %all-to-all-start) | async-done | bytes 393248 | tf_op jit(solution)/shard_map/all_to_all | solution.py:173
  46.1 3.6 %convolution_bitcast_fusion.4 = f32[96,1024]{1,0:T(8,128)S(1)} fusion(f32[8,96,128]{2,1,0:T(8,128)S(1)} %all-to-all-done, f32[8,128,1024]{2,1,0:T(8,128)} %constant.42.clone), kind=kOutput, calls=%fused_computation.7 | convolution fusion | flops 603979776 | bytes 4980736 | tf_op jit(solution)/shard_map/imy,iyq->mq/dot_general | solution.py:20
  50.6 0.3 multiply_add_fusion.6
  51.2 0.8 multiply_add_fusion.4
  52.1 1.5 %collective-permute-start.3 = (f32[3,32,2,512]{3,2,1,0:T(2,128)S(1)}, f32[3,32,2,512]{3,2,1,0:T(2,128)S(1)}, u32[]{:S(2)}, u32[]{:S(2)}) collective-permute-start(f32[3,32,2,512]{3,2,1,0:T(2,128)S(1)} %pad_maximum_fusion), channel_id=1, source_target_pairs={{0,8},{1,9},{2,10},{3,11},{4,12},{5,13},{6,14},{7,15},{16,24},{17,... | collective-permute-start | bytes 1179656 | tf_op jit(solution)/shard_map/ppermute | solution.py:184
  53.6 0.3 reshape.484
  54.0 0.8 collective-permute-done.3
  56.0 0.5 multiply_add_fusion.1
  56.8 0.3 reshape.495
  57.1 3.6 %convolution_bitcast_fusion.3 = f32[8,96,128]{2,1,0:T(8,128)S(1)} fusion(f32[96,1024,1]{1,0,2:T(8,128)S(1)} %reshape.495, f32[1024,8,128]{2,0,1:T(8,128)} %constant.47.clone), kind=kOutput, calls=%fused_computation.6 | convolution fusion | flops 603979776 | bytes 4980736 | tf_op jit(solution)/shard_map/mq,qiy->imy/dot_general | solution.py:20
  60.7 16.3 %all_to_all.10 = f32[8,96,128]{2,1,0:T(8,128)S(1)} all-to-all(f32[8,96,128]{2,1,0:T(8,128)S(1)} %convolution_bitcast_fusion.3), channel_id=1, replica_groups=mesh['group'=2,'tm'=2,'space'=8] {'space'}, dimensions={0} | all-to-all | bytes 786432 | tf_op jit(solution)/shard_map/all_to_all | solution.py:188
  77.1 0.5 reshape.486
  77.7 0.5 convolution_bitcast_fusion.2
  78.2 0.9 %copy-done.2 = f32[512,1024,1]{1,0,2:T(8,128)S(1)} copy-done((f32[512,1024,1]{1,0,2:T(8,128)S(1)}, f32[512,1024,1]{1,0,2:T(8,128)}, u32[]{:S(2)}) %copy-start.2) | copy-done | bytes 2097176
  79.1 2.8 %add_bitcast_fusion = f32[1,3,128,1024]{3,2,1,0:T(8,128)} fusion(f32[3,128,1024]{2,1,0:T(8,128)S(1)} %shard_map.145, f32[3,128,512]{2,1,0:T(8,128)S(1)} %convolution_bitcast_fusion.2, f32[512,1024,1]{1,0,2:T(8,128)S(1)} %copy-done.2), kind=kOutput, calls=%fused_computation | convolution fusion | flops 1208352768 | bytes 6029312 | tf_op jit(solution)/shard_map/fYk,kx->fYx/dot_general | solution.py:20
  (38 shorter events, 3.2 us)
Async XLA Ops:
  0.0 21.7 %copy-start.5 = (f32[64,128,1]{1,0,2:T(8,128)S(1)}, f32[64,128,1]{1,0,2:T(8,128)}, u32[]{:S(2)}) copy-start(f32[64,128,1]{1,0,2:T(8,128)} %constant.54) | copy-start | bytes 98308
  1.0 9.0 %collective-permute-start = (f32[3,8,1024]{2,1,0:T(8,128)S(1)}, f32[3,8,1024]{2,1,0:T(8,128)S(1)}, u32[]{:S(2)}, u32[]{:S(2)}) collective-permute-start(f32[3,8,1024]{2,1,0:T(8,128)S(1)} %get-tuple-element.6), channel_id=1, source_target_pairs={{0,1},{1,2},{2,3},{3,4},{4,5},{5,6},{6,7},{7,0},{8,9},{9,10},{10,1... | collective-permute-start | bytes 294920 | tf_op jit(solution)/shard_map/ppermute | solution.py:157
  4.0 6.7 %collective-permute-start.1 = (f32[3,8,1024]{2,1,0:T(8,128)S(1)}, f32[3,8,1024]{2,1,0:T(8,128)S(1)}, u32[]{:S(2)}, u32[]{:S(2)}) collective-permute-start(f32[3,8,1024]{2,1,0:T(8,128)S(1)} %get-tuple-element.5), channel_id=1, source_target_pairs={{1,0},{2,1},{3,2},{4,3},{5,4},{6,5},{7,6},{0,7},{9,8},{10,9},{11,1... | collective-permute-start | bytes 294920 | tf_op jit(solution)/shard_map/ppermute | solution.py:158
  10.7 1.4 %copy-start = (f32[1,3,128,1024]{3,2,1,0:T(8,128)S(1)}, f32[1,3,128,1024]{3,2,1,0:T(8,128)}, u32[]{:S(2)}) copy-start(f32[1,3,128,1024]{3,2,1,0:T(8,128)} %param.15) | copy-start | bytes 4718596
  12.1 10.2 %copy-start.1 = (f32[2,256,1024,1]{2,1,3,0:T(8,128)S(1)}, f32[2,256,1024,1]{2,1,3,0:T(8,128)}, u32[]{:S(2)}) copy-start(f32[2,256,1024,1]{2,1,3,0:T(8,128)} %constant.53) | copy-start | bytes 6291460
  23.5 3.1 %collective-permute-start.2 = (f32[2,256,3,64]{1,3,2,0:T(8,128)S(1)}, f32[2,256,3,64]{1,3,2,0:T(8,128)S(1)}, u32[]{:S(2)}, u32[]{:S(2)}) collective-permute-start(f32[2,256,3,64]{1,3,2,0:T(8,128)S(1)} %fusion.26), channel_id=1, source_target_pairs={{0,8},{1,9},{2,10},{3,11},{4,12},{5,13},{6,14},{7,15},{16,24},{17,... | collective-permute-start | bytes 1179656 | tf_op jit(solution)/shard_map/ppermute | solution.py:169
  25.4 1.2 %copy-start.3 = (f32[2,256,512,1]{2,1,3,0:T(8,128)S(1)}, f32[2,256,512,1]{2,1,3,0:T(8,128)}, u32[]{:S(2)}) copy-start(f32[2,256,512,1]{2,1,3,0:T(8,128)} %constant.55) | copy-start | bytes 3145732
  25.4 1.3 %copy-start.4 = (f32[3,64,512]{2,1,0:T(8,128)S(1)}, f32[3,64,512]{2,1,0:T(8,128)}, u32[]{:S(2)}) copy-start(f32[3,64,512]{2,1,0:T(8,128)} %param.16) | copy-start | bytes 1179652
  27.4 7.1 %copy-start.8 = (f32[256]{0:T(256)S(1)}, f32[256]{0:T(256)}, u32[]{:S(2)}) copy-start(f32[256]{0:T(256)} %constant.43.clone) | copy-start | bytes 3076
  29.5 16.7 %all-to-all-start = ((f32[8,96,128]{2,1,0:T(8,128)}), f32[8,96,128]{2,1,0:T(8,128)S(1)}, u32[]{:S(2)}, u32[]{:S(2)}) async-start(f32[8,96,128]{2,1,0:T(8,128)} %reshape.483), calls=%async_computation | async-start | bytes 786432 | tf_op jit(solution)/shard_map/all_to_all | solution.py:173
  49.7 0.9 %copy-start.6 = (f32[512]{0:T(512)S(1)}, f32[512]{0:T(512)}, u32[]{:S(2)}) copy-start(f32[512]{0:T(512)} %constant.52) | copy-start | bytes 6148
  52.1 2.6 %collective-permute-start.3 = (f32[3,32,2,512]{3,2,1,0:T(2,128)S(1)}, f32[3,32,2,512]{3,2,1,0:T(2,128)S(1)}, u32[]{:S(2)}, u32[]{:S(2)}) collective-permute-start(f32[3,32,2,512]{3,2,1,0:T(2,128)S(1)} %pad_maximum_fusion), channel_id=1, source_target_pairs={{0,8},{1,9},{2,10},{3,11},{4,12},{5,13},{6,14},{7,15},{16,24},{17,... | collective-permute-start | bytes 1179656 | tf_op jit(solution)/shard_map/ppermute | solution.py:184
  60.7 16.9 %copy-start.7 = (f32[64,128,1]{1,0,2:T(8,128)S(1)}, f32[64,128,1]{1,0,2:T(8,128)}, u32[]{:S(2)}) copy-start(f32[64,128,1]{1,0,2:T(8,128)} %constant.56) | copy-start | bytes 98308
  77.5 1.6 %copy-start.2 = (f32[512,1024,1]{1,0,2:T(8,128)S(1)}, f32[512,1024,1]{1,0,2:T(8,128)}, u32[]{:S(2)}) copy-start(f32[512,1024,1]{1,0,2:T(8,128)} %constant.57) | copy-start | bytes 6291460

commit v2 on v1

--- a/solution.py
+++ b/solution.py
@@ -1,3 +1,4 @@
+import functools
 import math
 
 import jax
@@ -13,11 +14,26 @@
 TIME_STEP = 0.25
 CORIOLIS = 0.5
 HALO = 8
+MESH = pl.DeviceIdType.MESH
 HIGH = lax.Precision.HIGH
 
 
 def dot(spec, a, b):
     return jnp.einsum(spec, a, b, precision=HIGH, preferred_element_type=jnp.float32)
+
+
+def halves(table):
+    high = table.astype(jnp.bfloat16)
+    return high, (table - high.astype(np.float32)).astype(jnp.bfloat16)
+
+
+def split_dot(spec, a, table):
+    high = lax.reduce_precision(a, 8, 7)
+    low = (a - high).astype(jnp.bfloat16)
+    high = high.astype(jnp.bfloat16)
+    table_high, table_low = halves(table)
+    one = lambda x, t: jnp.einsum(spec, x, t, preferred_element_type=jnp.float32)
+    return one(high, table_high) + (one(low, table_high) + one(high, table_low))
 
 
 def tables(nc, parts):
@@ -71,21 +87,52 @@
     return mid, (-0.5 * flux, rate_u, rate_v)
 
 
-def heun_kernel(before, state, after, fine, now, first):
+def rows_at(row):
+    return row if isinstance(row, int) else pl.multiple_of(row, 8)
+
+
+def greet(peers):
+    barrier = pltpu.get_barrier_semaphore()
+    for peer in peers:
+        pl.semaphore_signal(barrier, inc=1, device_id={"space": peer}, device_id_type=MESH)
+    pl.semaphore_wait(barrier, len(peers))
+
+
+def heun_kernel(size, state, fine, now, first, send, recv):
     rows = state.shape[1]
     blocks = (rows + 2 * HALO) // 8
+    me = lax.axis_index("space")
+    after, before = lax.rem(me + 1, size), lax.rem(me + size - 1, size)
+    greet((after, before))
+    copies = [
+        pltpu.make_async_remote_copy(
+            src_ref=state.at[:, pl.ds(source, HALO)],
+            dst_ref=now.at[:, pl.ds(target, HALO)],
+            send_sem=send.at[n],
+            recv_sem=recv.at[n],
+            device_id={"space": peer},
+            device_id_type=MESH,
+        )
+        for n, (source, target, peer) in enumerate(
+            ((rows - HALO, 8, after), (0, 16 + rows, before))
+        )
+    ]
+    for copy in copies:
+        copy.start()
+    pad = jnp.zeros((HALO, state.shape[2]), jnp.float32)
     for f in range(3):
-        now[f, 8:16] = before[f]
         now[f, 16 : 16 + rows] = state[f]
-        now[f, 16 + rows : 24 + rows] = after[f]
+        for ref in (now, first):
+            ref[f, 0:8] = pad
+            ref[f, 24 + rows : 32 + rows] = pad
 
     def window(ref, block):
-        at = pl.multiple_of(block * 8, 8)
+        at = rows_at(block * 8)
         return [ref[f, pl.ds(at, 24)] for f in range(3)]
 
     def predict(block, _):
         mid, rate = tendency(window(now, block))
-        at = pl.multiple_of(block * 8 + 8, 8)
+        at = rows_at(block * 8 + 8)
         for f in range(3):
             first[f, pl.ds(at, 8)] = mid[f] + TIME_STEP * rate[f]
         return 0
@@ -93,8 +140,8 @@
     def correct(out, shift):
         def body(block, _):
             mid, rate = tendency(window(first, block))
-            at = pl.multiple_of(block * 8 + 8, 8)
-            to = pl.multiple_of(block * 8 + 8 - shift, 8)
+            at = rows_at(block * 8 + 8)
+            to = rows_at(block * 8 + 8 - shift)
             for f in range(3):
                 out[f, pl.ds(to, 8)] = 0.5 * (now[f, pl.ds(at, 8)] + mid[f] + TIME_STEP * rate[f])
             return 0
@@ -102,28 +149,79 @@
         return body
 
     for step in range(STEPS):
-        lax.fori_loop(0, blocks, predict, 0)
+        if step == 0:
+            lax.fori_loop(2, blocks - 2, predict, 0)
+            for copy in copies:
+                copy.wait()
+            for block in (0, 1, blocks - 2, blocks - 1):
+                predict(block, 0)
+        else:
+            lax.fori_loop(0, blocks, predict, 0)
         if step < STEPS - 1:
             lax.fori_loop(0, blocks, correct(now, 0), 0)
         else:
             lax.fori_loop(1, blocks - 1, correct(fine, 16), 0)
 
 
-def heun(before, state, after):
+def heun(state, size):
     fields, rows, width = state.shape
     vmem = pl.BlockSpec(memory_space=pltpu.VMEM)
     padded = pltpu.VMEM((fields, rows + 4 * HALO, width), jnp.float32)
     return pl.pallas_call(
-        heun_kernel,
+        functools.partial(heun_kernel, size),
         out_shape=jax.ShapeDtypeStruct(state.shape, jnp.float32),
-        in_specs=[vmem] * 3,
+        in_specs=[vmem],
         out_specs=vmem,
-        scratch_shapes=[padded, padded],
-        compiler_params=pltpu.CompilerParams(vmem_limit_bytes=24 << 20),
+        scratch_shapes=[padded, padded] + [pltpu.SemaphoreType.DMA((2,))] * 2,
+        compiler_params=pltpu.CompilerParams(
+            collective_id=0, has_side_effects=True, vmem_limit_bytes=24 << 20
+        ),
         cost_estimate=pl.CostEstimate(
             flops=200 * rows * width, bytes_accessed=24 * rows * width, transcendentals=0
         ),
-    )(before, state, after)
+    )(state)
+
+
+def exchange_kernel(size, blocks, out, landed, send, recv):
+    me = lax.axis_index("space")
+    peers = [lax.rem(me + d, size) for d in range(1, size)]
+    greet(peers)
+    copies = [
+        pltpu.make_async_remote_copy(
+            src_ref=blocks.at[peer],
+            dst_ref=landed.at[me],
+            send_sem=send.at[n],
+            recv_sem=recv.at[n],
+            device_id={"space": peer},
+            device_id_type=MESH,
+        )
+        for n, peer in enumerate(peers)
+    ]
+    for copy in copies:
+        copy.start()
+    out[me] = blocks[me]
+    for n, copy in enumerate(copies):
+        copy.wait()
+        origin = lax.rem(me + size - 1 - n, size)
+        out[origin] = landed[origin]
+
+
+def exchange(blocks, size, number):
+    vmem = pl.BlockSpec(memory_space=pltpu.VMEM)
+    return pl.pallas_call(
+        functools.partial(exchange_kernel, size),
+        out_shape=jax.ShapeDtypeStruct(blocks.shape, jnp.float32),
+        in_specs=[vmem],
+        out_specs=vmem,
+        scratch_shapes=[pltpu.VMEM(blocks.shape, jnp.float32)]
+        + [pltpu.SemaphoreType.DMA((size - 1,))] * 2,
+        compiler_params=pltpu.CompilerParams(
+            collective_id=number, has_side_effects=True, vmem_limit_bytes=16 << 20
+        ),
+        cost_estimate=pl.CostEstimate(
+            flops=0, bytes_accessed=30 * blocks.size, transcendentals=0
+        ),
+    )(blocks)
 
 
 def apply_operator(s, wave_east, wave_north):
@@ -145,24 +243,19 @@
 def shards(start_old, incoming):
     size, slices = lax.axis_size("space"), lax.axis_size("tm")
     state = start_old[0]
-    _, fine_rows, width = state.shape
+    width = state.shape[2]
     rows, nc = incoming.shape[1:]
     half = nc // 2
     count = half // size
     forward, wide, along, back, inverse, wave, sine, versine = tables(nc, size)
     pairs = np.repeat(np.eye(rows, dtype=np.float32), RATIO, axis=1)
 
-    up = [(i, (i + 1) % size) for i in range(size)]
-    down = [(j, i) for i, j in up]
-    before = lax.ppermute(state[:, fine_rows - HALO :], "space", up)
-    after = lax.ppermute(state[:, :HALO], "space", down)
-
     is_first = (lax.axis_index("tm") == 0).astype(jnp.float32)
     start_rows = dot("yY,fYx->fyx", 0.5 * pairs, state)
     drift = dot("ckx,fyx->ckfy", wide, start_rows)
     drift = drift - dot("ckx,fyx->ckfy", forward, is_first * incoming)
 
-    fine = heun(before, state, after)
+    fine = heun(state, size)
     coarse_rows = dot("yY,fYx->fyx", 0.5 * pairs, fine)
     coarse = dot("ckx,fyx->ckfy", wide, coarse_rows)
     route = [(i, i + 1) for i in range(slices - 1)]
@@ -170,8 +263,8 @@
 
     gap = gap.reshape(2, size, count, 3, rows).transpose(1, 3, 2, 0, 4)
     gap = gap.reshape(size, 3 * count, 2 * rows)
-    piece = lax.all_to_all(gap, "space", 0, 0)
-    spectra = dot("imy,iyq->mq", piece, along.reshape(size, 2 * rows, 2 * nc))
+    piece = exchange(gap, size, 1)
+    spectra = split_dot("imy,iyq->mq", piece, along.reshape(size, 2 * rows, 2 * nc))
     spectra = spectra.reshape(3, count, 2, nc)
 
     mine = lax.axis_index("space") * count
@@ -184,8 +277,8 @@
         change = propagate(spectra + lax.ppermute(change, "tm", route), *factors)
 
     change = change.reshape(3 * count, 2 * nc)
-    moved = dot("mq,qiy->imy", change, back.reshape(2 * nc, size, 2 * rows))
-    moved = lax.all_to_all(moved, "space", 0, 0)
+    moved = split_dot("mq,qiy->imy", change, back.reshape(2 * nc, size, 2 * rows))
+    moved = exchange(moved, size, 2)
     moved = moved.reshape(size, 3, count, 2, rows).transpose(1, 4, 3, 0, 2)
     moved = moved.reshape(3, rows, nc)
     moved = dot("yY,fyk->fYk", pairs, moved)

time: 82.5 us -> 70.3 us (0.85)
  Pallas kernels: 9.59 us -> 39.1 us
  blocking collectives: 16.3 us -> 0 us
  waiting for transfers between devices: 15.1 us -> 0.79 us
  starting transfers between devices: 13.9 us -> 3.54 us
  local copies, waits for them, and re-layouts: 8.38 us -> 7.26 us
    pallas_call x1 -> x3, Pallas kernels: 9.59 us -> 39.1 us  [the longest x2 22.3 us: exchange(): pl.pallas_call(functools.partial(exchange_kernel, size), out_shape=jax.Sh...]
    all_to_all x1 -> x0, blocking collectives: 16.3 us -> none  [shards(): moved = lax.all_to_all(moved, 'space', 0, 0)]
    all_to_all x1 -> x0, waiting for transfers between devices: 10.7 us -> none  [shards(): piece = lax.all_to_all(gap, 'space', 0, 0)]
    ppermute x2 -> x0, starting transfers between devices: 6.12 us -> none  [the longest x1 3.1 us: shards(): after = lax.ppermute(state[:, :HALO], 'space', down)]
    all_to_all x1 -> x0, starting transfers between devices: 4.96 us -> none  [shards(): piece = lax.all_to_all(gap, 'space', 0, 0)]
    dot_general x0 -> x6, matrix products: none -> 4.42 us  [split_dot(): jnp.einsum(spec, x, t, preferred_element_type=jnp.float32)]
    dot_general x9 -> x7, matrix products: 14.6 us -> 10.3 us  [dot(): jnp.einsum(spec, a, b, precision=HIGH, preferred_element_type=jnp.float32)]
    ppermute x2 -> x0, waiting for transfers between devices: 3.62 us -> none  [the longest x1 2.83 us: shards(): before = lax.ppermute(state[:, fine_rows - HALO:], 'space', up)]
  transfers between devices with their start and end apart: 5 -> 2, of which waited for: 4 -> 1; matrix products, arithmetic and copies ran while one was open for 4% -> 7% of each run, Pallas kernels for 0% -> 0%
where the time goes in v2:
time: 70.3 us; the launch traced here: 69.3 us
  Pallas kernels  39.1 us (56%)
  matrix products  14.7 us (21%)
  local copies, waits for them, and re-layouts  7.26 us (10%)
  other arithmetic  3.6 us (5%)
  starting transfers between devices  3.54 us (5%)
  waiting for transfers between devices  0.79 us (1%)
    pallas_call x2, Pallas kernels, exchange(): pl.pallas_call(functools.partial(exchange_kernel, size), out_shape=jax.Sh...  22.3 us
    pallas_call x1, Pallas kernels, heun(): pl.pallas_call(functools.partial(heun_kernel, size), out_shape=jax.ShapeD...  16.8 us
    dot_general x7, matrix products, dot(): jnp.einsum(spec, a, b, precision=HIGH, preferred_element_type=jnp.float32)  10.3 us
    dot_general x6, matrix products, split_dot(): jnp.einsum(spec, x, t, preferred_element_type=jnp.float32)  4.42 us
    unnamed x23, local copies, waits for them, and re-layouts  3.38 us
    ppermute x1, starting transfers between devices, shards(): gap = lax.ppermute(coarse, 'tm', route) - drift  2.05 us
    add x3, other arithmetic, propagate(): a + sine * b + versine * c  1.62 us
    ppermute x1, starting transfers between devices, shards(): change = propagate(spectra + lax.ppermute(change, 'tm', route), *factors)  1.49 us
  transfers between devices with their start and end apart: 2, of which 1 were waited for; matrix products, arithmetic and copies ran while one was open for 7% of the time, Pallas kernels for 0%

profile of v2, /device:TPU:0, one launch (start us, length us, event | category | flops | bytes accessed | tf_op | source)
XLA Modules:
  0.0 69.3 jit_solution(3084411235045246207)
XLA Ops:
  0.0 1.4 %copy-done = f32[1,3,128,1024]{3,2,1,0:T(8,128)S(1)} copy-done((f32[1,3,128,1024]{3,2,1,0:T(8,128)S(1)}, f32[1,3,128,1024]{3,2,1,0:T(8,128)}, u32[]{:S(2)}) %copy-start) | copy-done | bytes 1572888
  1.4 16.8 %shard_map.181 = f32[3,128,1024]{2,1,0:T(8,128)S(1)} custom-call(f32[3,128,1024]{2,1,0:T(8,128)S(1)} %bitcast.129), custom_call_target="tpu_custom_call" | custom-call | flops 26214400 | bytes 3145728 | tf_op jit(solution)/shard_map/pallas_call | solution.py:170
  18.2 0.5 convolution_bitcast_fusion.1
  18.7 1.2 %fusion.37 = f32[2,256,3,64]{1,3,2,0:T(8,128)S(1)} fusion(f32[2,256,1024,1]{2,1,3,0:T(8,128)S(1)} %copy-done.3, f32[3,64,1024,1]{2,1,0,3:T(8,128)S(1)} %convolution_bitcast_fusion.1), kind=kOutput, calls=%fused_computation.90 | convolution fusion | flops 603979776 | bytes 3276800 | tf_op jit(solution)/shard_map/ckx,fyx->ckfy/dot_general | solution.py:22
  19.9 2.0 %collective-permute-start = (f32[2,256,3,64]{1,3,2,0:T(8,128)S(1)}, f32[2,256,3,64]{1,3,2,0:T(8,128)}, u32[]{:S(2)}, u32[]{:S(2)}) collective-permute-start(f32[2,256,3,64]{1,3,2,0:T(8,128)S(1)} %fusion.37), channel_id=1, source_target_pairs={{0,8},{1,9},{2,10},{3,11},{4,12},{5,13},{6,14},{7,15},{16,24},{17,... | collective-permute-start | bytes 1179656 | tf_op jit(solution)/shard_map/ppermute | solution.py:262
  22.0 0.6 convolution_bitcast_fusion
  22.7 0.9 %constant_dynamic-slice_fusion = (f32[32,512]{1,0:T(8,128)S(1)}, f32[32,512]{1,0:T(8,128)S(1)}) fusion(f32[256,512]{1,0:T(8,128)} %constant.50.clone, s32[]{:T(128)S(6)} %select_n.2, f32[256,512]{1,0:T(8,128)} %constant.49.clone), kind=kLoop, calls=%fused_computation.80 | loop fusion | bytes 262148 | tf_op jit(solution)/shard_map/dynamic_slice | solution.py:271
  23.6 2.8 %fusion.38 = f32[3,64,2,256]{3,1,0,2:T(8,128)S(1)} fusion(f32[3,64,1024,1]{2,1,0,3:T(8,128)S(1)} %convolution_bitcast_fusion, f32[2,256,1024,1]{2,1,3,0:T(8,128)} %constant.59), kind=kOutput, calls=%fused_computation.91 | convolution fusion | flops 603979776 | bytes 3276800 | tf_op jit(solution)/shard_map/ckx,fyx->ckfy/dot_general | solution.py:22
  26.4 2.0 %fusion.2 = f32[2,256,3,64]{1,3,2,0:T(8,128)S(1)} fusion(f32[2,256,3,64]{1,3,2,0:T(8,128)} %collective-permute-done, f32[3,64,2,256]{3,1,0,2:T(8,128)S(1)} %fusion.38, f32[2,256,512,1]{2,1,3,0:T(8,128)} %constant.61, f32[3,64,512]{2,1,0:T(8,128)S(1)} %copy-done.6, f32[]{:T(128)S(6)} %convert_element_type.15), kind=kOutput, calls=%fused_computation.12 | convolution fusion | flops 302284800 | bytes 2621444 | tf_op jit(solution)/shard_map/ckx,fyx->ckfy/dot_general | solution.py:22
  28.7 0.6 copy.26
  29.3 0.4 reshape.483.blocks
  29.8 10.3 %shard_map.182 = f32[8,96,128]{2,1,0:T(8,128)S(1)} custom-call(f32[8,96,128]{2,1,0:T(8,128)S(1)} %reshape.483.blocks), custom_call_target="tpu_custom_call" | custom-call | bytes 2949120 | tf_op jit(solution)/shard_map/pallas_call | solution.py:211
  40.1 2.1 %convolution_bitcast_fusion.3 = f32[96,1024]{1,0:T(8,128)S(1)} fusion(bf16[8,128,1024]{2,1,0:T(8,128)(2,1)} %constant.47.clone, f32[8,96,128]{2,1,0:T(8,128)S(1)} %shard_map.182), kind=kOutput, calls=%fused_computation.7 | convolution fusion | flops 201523200 | bytes 2883584 | tf_op jit(solution)/shard_map/imy,iyq->mq/dot_general | solution.py:35
  42.2 0.5 fusion.4
  42.6 0.5 fusion.3
  44.0 0.3 multiply_add_fusion.6
  44.6 0.8 %multiply_add_fusion.4 = (f32[1,32,2,512]{3,2,1,0:T(2,128)S(1)}, f32[1,32,2,512]{3,2,1,0:T(2,128)S(1)}, f32[1,32,2,512]{3,2,1,0:T(2,128)S(1)}) fusion(f32[1,32,2,512]{3,2,1,0:T(2,128)S(1)} %unstack.61, f32[32]{0:T(128)S(1)} %dynamic_slice.10, f32[32,512]{1,0:T(8,128)S(1)} %get-tuple-element.35, f32[32,512]{1,0:T(8,128)S(1)} %get-tuple-element.36, ...), kind=kLoop, calls=%fused_computation.58 | loop fusion | flops 917504 | bytes 1378432 | tf_op jit(solution)/shard_map/add | solution.py:240
  45.5 1.5 %collective-permute-start.1 = (f32[3,32,2,512]{3,2,1,0:T(2,128)S(1)}, f32[3,32,2,512]{3,2,1,0:T(2,128)S(1)}, u32[]{:S(2)}, u32[]{:S(2)}) collective-permute-start(f32[3,32,2,512]{3,2,1,0:T(2,128)S(1)} %pad_maximum_fusion), channel_id=1, source_target_pairs={{0,8},{1,9},{2,10},{3,11},{4,12},{5,13},{6,14},{7,15},{16,24},{17,... | collective-permute-start | bytes 1179656 | tf_op jit(solution)/shard_map/ppermute | solution.py:277
  47.0 0.3 reshape.484
  47.4 0.8 %collective-permute-done.1 = f32[3,32,2,512]{3,2,1,0:T(2,128)S(1)} collective-permute-done((f32[3,32,2,512]{3,2,1,0:T(2,128)S(1)}, f32[3,32,2,512]{3,2,1,0:T(2,128)S(1)}, u32[]{:S(2)}, u32[]{:S(2)}) %collective-permute-start.1) | collective-permute-done | bytes 393248 | tf_op jit(solution)/shard_map/ppermute | solution.py:277
  48.6 0.3 fusion.22
  49.1 0.3 fusion.18
  49.4 0.5 multiply_add_fusion.1
  50.3 0.4 fusion.13
  50.7 0.9 %copy-done.5 = bf16[1024,8,128]{2,0,1:T(8,128)(2,1)S(1)} copy-done((bf16[1024,8,128]{2,0,1:T(8,128)(2,1)S(1)}, bf16[1024,8,128]{2,0,1:T(8,128)(2,1)}, u32[]{:S(2)}) %copy-start.5) | copy-done | bytes 2097176
  51.6 0.5 convolution_add_fusion
  52.1 0.5 fusion.blocks
  52.6 12.0 %shard_map.183 = f32[8,96,128]{2,1,0:T(8,128)S(1)} custom-call(f32[8,96,128]{2,1,0:T(8,128)S(1)} %fusion.blocks), custom_call_target="tpu_custom_call" | custom-call | bytes 2949120 | tf_op jit(solution)/shard_map/pallas_call | solution.py:211
  64.6 0.5 reshape.486
  65.2 0.5 convolution_bitcast_fusion.2
  65.7 0.9 %copy-done.4 = f32[512,1024,1]{1,0,2:T(8,128)S(1)} copy-done((f32[512,1024,1]{1,0,2:T(8,128)S(1)}, f32[512,1024,1]{1,0,2:T(8,128)}, u32[]{:S(2)}) %copy-start.4) | copy-done | bytes 2097176
  66.7 2.7 %add_bitcast_fusion = f32[1,3,128,1024]{3,2,1,0:T(8,128)} fusion(f32[3,128,1024]{2,1,0:T(8,128)S(1)} %shard_map.181, f32[3,128,512]{2,1,0:T(8,128)S(1)} %convolution_bitcast_fusion.2, f32[512,1024,1]{1,0,2:T(8,128)S(1)} %copy-done.4), kind=kOutput, calls=%fused_computation | convolution fusion | flops 1208352768 | bytes 6029312 | tf_op jit(solution)/shard_map/fYk,kx->fYx/dot_general | solution.py:22
  (40 shorter events, 2.6 us)
Async XLA Ops:
  0.0 18.2 %copy-start.7 = (f32[64,128,1]{1,0,2:T(8,128)S(1)}, f32[64,128,1]{1,0,2:T(8,128)}, u32[]{:S(2)}) copy-start(f32[64,128,1]{1,0,2:T(8,128)} %constant.60) | copy-start | bytes 98308
  0.0 1.4 %copy-start = (f32[1,3,128,1024]{3,2,1,0:T(8,128)S(1)}, f32[1,3,128,1024]{3,2,1,0:T(8,128)}, u32[]{:S(2)}) copy-start(f32[1,3,128,1024]{3,2,1,0:T(8,128)} %param.19) | copy-start | bytes 4718596
  1.4 17.3 %copy-start.3 = (f32[2,256,1024,1]{2,1,3,0:T(8,128)S(1)}, f32[2,256,1024,1]{2,1,3,0:T(8,128)}, u32[]{:S(2)}) copy-start(f32[2,256,1024,1]{2,1,3,0:T(8,128)} %constant.59) | copy-start | bytes 6291460
  18.7 3.9 %copy-start.10 = (f32[256]{0:T(256)S(1)}, f32[256]{0:T(256)}, u32[]{:S(2)}) copy-start(f32[256]{0:T(256)} %constant.48.clone) | copy-start | bytes 3076
  19.9 6.5 %collective-permute-start = (f32[2,256,3,64]{1,3,2,0:T(8,128)S(1)}, f32[2,256,3,64]{1,3,2,0:T(8,128)}, u32[]{:S(2)}, u32[]{:S(2)}) collective-permute-start(f32[2,256,3,64]{1,3,2,0:T(8,128)S(1)} %fusion.37), channel_id=1, source_target_pairs={{0,8},{1,9},{2,10},{3,11},{4,12},{5,13},{6,14},{7,15},{16,24},{17,... | collective-permute-start | bytes 1179656 | tf_op jit(solution)/shard_map/ppermute | solution.py:262
  22.6 3.8 %copy-start.6 = (f32[3,64,512]{2,1,0:T(8,128)S(1)}, f32[3,64,512]{2,1,0:T(8,128)}, u32[]{:S(2)}) copy-start(f32[3,64,512]{2,1,0:T(8,128)} %param.20) | copy-start | bytes 1179652
  29.8 12.4 %copy-start.2 = (bf16[8,128,1024]{2,1,0:T(8,128)(2,1)S(1)}, bf16[8,128,1024]{2,1,0:T(8,128)(2,1)}, u32[]{:S(2)}) copy-start(bf16[8,128,1024]{2,1,0:T(8,128)(2,1)} %constant.46.clone) | copy-start | bytes 6291460
  43.1 0.9 %copy-start.8 = (f32[512]{0:T(512)S(1)}, f32[512]{0:T(512)}, u32[]{:S(2)}) copy-start(f32[512]{0:T(512)} %constant.58) | copy-start | bytes 6148
  45.5 2.6 %collective-permute-start.1 = (f32[3,32,2,512]{3,2,1,0:T(2,128)S(1)}, f32[3,32,2,512]{3,2,1,0:T(2,128)S(1)}, u32[]{:S(2)}, u32[]{:S(2)}) collective-permute-start(f32[3,32,2,512]{3,2,1,0:T(2,128)S(1)} %pad_maximum_fusion), channel_id=1, source_target_pairs={{0,8},{1,9},{2,10},{3,11},{4,12},{5,13},{6,14},{7,15},{16,24},{17,... | collective-permute-start | bytes 1179656 | tf_op jit(solution)/shard_map/ppermute | solution.py:277
  48.6 1.7 %copy-start.1 = (bf16[1024,8,128]{2,0,1:T(8,128)(2,1)S(1)}, bf16[1024,8,128]{2,0,1:T(8,128)(2,1)}, u32[]{:S(2)}) copy-start(bf16[1024,8,128]{2,0,1:T(8,128)(2,1)} %constant.52.clone) | copy-start | bytes 6291460
  50.0 1.6 %copy-start.5 = (bf16[1024,8,128]{2,0,1:T(8,128)(2,1)S(1)}, bf16[1024,8,128]{2,0,1:T(8,128)(2,1)}, u32[]{:S(2)}) copy-start(bf16[1024,8,128]{2,0,1:T(8,128)(2,1)} %constant.53.clone) | copy-start | bytes 6291460
  52.6 12.6 %copy-start.9 = (f32[64,128,1]{1,0,2:T(8,128)S(1)}, f32[64,128,1]{1,0,2:T(8,128)}, u32[]{:S(2)}) copy-start(f32[64,128,1]{1,0,2:T(8,128)} %constant.62) | copy-start | bytes 98308
  65.1 1.6 %copy-start.4 = (f32[512,1024,1]{1,0,2:T(8,128)S(1)}, f32[512,1024,1]{1,0,2:T(8,128)}, u32[]{:S(2)}) copy-start(f32[512,1024,1]{1,0,2:T(8,128)} %constant.63) | copy-start | bytes 6291460

commit v3 on v2

--- a/solution.py
+++ b/solution.py
@@ -15,11 +15,6 @@
 CORIOLIS = 0.5
 HALO = 8
 MESH = pl.DeviceIdType.MESH
-HIGH = lax.Precision.HIGH
-
-
-def dot(spec, a, b):
-    return jnp.einsum(spec, a, b, precision=HIGH, preferred_element_type=jnp.float32)
 
 
 def halves(table):
@@ -27,13 +22,14 @@
     return high, (table - high.astype(np.float32)).astype(jnp.bfloat16)
 
 
-def split_dot(spec, a, table):
-    high = lax.reduce_precision(a, 8, 7)
-    low = (a - high).astype(jnp.bfloat16)
-    high = high.astype(jnp.bfloat16)
-    table_high, table_low = halves(table)
-    one = lambda x, t: jnp.einsum(spec, x, t, preferred_element_type=jnp.float32)
-    return one(high, table_high) + (one(low, table_high) + one(high, table_low))
+def split(a):
+    high = a.astype(jnp.bfloat16)
+    return high, (a - high.astype(jnp.float32)).astype(jnp.bfloat16)
+
+
+def dot(a, b, sides=(1, 0)):
+    dims = (((sides[0],), (sides[1],)), ((), ()))
+    return lax.dot_general(a, b, dims, preferred_element_type=jnp.float32)
 
 
 def tables(nc, parts):
@@ -174,7 +170,7 @@
         out_specs=vmem,
         scratch_shapes=[padded, padded] + [pltpu.SemaphoreType.DMA((2,))] * 2,
         compiler_params=pltpu.CompilerParams(
-            collective_id=0, has_side_effects=True, vmem_limit_bytes=24 << 20
+            collective_id=0, has_side_effects=True, vmem_limit_bytes=8 << 20
         ),
         cost_estimate=pl.CostEstimate(
             flops=200 * rows * width, bytes_accessed=24 * rows * width, transcendentals=0
@@ -182,107 +178,206 @@
     )(state)
 
 
-def exchange_kernel(size, blocks, out, landed, send, recv):
-    me = lax.axis_index("space")
+def apply_operator(s, a, b):
+    (hr, hi), (ur, ui), (vr, vi) = s
+    return (
+        (a * ui + b * vi, -(a * ur + b * vr)),
+        (a * hi + CORIOLIS * vr, CORIOLIS * vi - a * hr),
+        (b * hi - CORIOLIS * ur, -(b * hr) - CORIOLIS * ui),
+    )
+
+
+def coarse_kernel(
+    size, slices, fine, state, incoming, pairs, wide_h, wide_l, short_h, short_l,
+    east, north, sine, versine, along_h, along_l, back_h, back_l, out,
+    mine, theirs, gap, landed, acc, change, relayed, leaving, returned,
+    ah, al, bh, bl, fetch, x_send, x_recv, y_send, y_recv, t_send, t_recv,
+):
+    fields, rows, nc = incoming.shape
+    half = nc // 2
+    count = half // size
+    me, slot = lax.axis_index("space"), lax.axis_index("tm")
     peers = [lax.rem(me + d, size) for d in range(1, size)]
-    greet(peers)
+    origins = [lax.rem(me + size - d, size) for d in range(1, size)]
+    following, previous = lax.rem(slot + 1, slices), lax.rem(slot + slices - 1, slices)
+
+    fetches = [
+        pltpu.make_async_copy(source, target, fetch.at[n])
+        for n, (source, target) in enumerate(
+            ((along_h, ah), (along_l, al), (back_h, bh), (back_l, bl))
+        )
+    ]
+    for copy in fetches:
+        copy.start()
+
+    barrier = pltpu.get_barrier_semaphore()
+    for peer in peers:
+        pl.semaphore_signal(barrier, inc=1, device_id={"space": peer}, device_id_type=MESH)
+    for other in (following, previous):
+        pl.semaphore_signal(barrier, inc=1, device_id={"tm": other}, device_id_type=MESH)
+
+    def to_space(source, target, send, recv, peer):
+        return pltpu.make_async_remote_copy(
+            src_ref=source, dst_ref=target, send_sem=send, recv_sem=recv,
+            device_id={"space": peer}, device_id_type=MESH,
+        )
+
+    def to_next(source, target, n):
+        return pltpu.make_async_remote_copy(
+            src_ref=source, dst_ref=target, send_sem=t_send.at[n], recv_sem=t_recv.at[n],
+            device_id={"tm": following}, device_id_type=MESH,
+        )
+
+    def spectra_of(stacked, high, low):
+        up, down = split(stacked)
+        return dot(high, up, (1, 1)) + (dot(high, down, (1, 1)) + dot(low, up, (1, 1)))
+
+    def x_spectra(ref):
+        parts = [split(ref[f]) for f in range(fields)]
+        averaged = [dot(pairs[...], up) + dot(pairs[...], down) for up, down in parts]
+        return spectra_of(jnp.concatenate(averaged, 0), wide_h[...], wide_l[...])
+
+    def lay_out(value, put):
+        for f in range(fields):
+            both = value[:, f * rows : (f + 1) * rows]
+            both = jnp.concatenate([both[:half], both[half:]], 1)
+            for j in range(size):
+                put(j, slice(f * count, (f + 1) * count), both[j * count : (j + 1) * count])
+
+    def put_mine(j, at, value):
+        mine[j, at] = value
+
+    def put_gap(j, at, value):
+        gap[j, at] = value
+
+    lay_out(x_spectra(fine), put_mine)
+    pl.semaphore_wait(barrier, len(peers) + 2)
+    ahead = to_next(mine, theirs, 0)
+    ahead.start()
+    fresh = jnp.concatenate([incoming[f] for f in range(fields)], 0)
+    fresh = spectra_of(fresh, short_h[...], short_l[...])
+    drift = x_spectra(state) - jnp.where(slot == 0, fresh, 0.0)
+    lay_out(-drift, put_gap)
+    ahead.wait()
+    for j in range(size):
+        gap[j] = gap[j] + jnp.where(slot == 0, 0.0, theirs[j])
+
     copies = [
-        pltpu.make_async_remote_copy(
-            src_ref=blocks.at[peer],
-            dst_ref=landed.at[me],
-            send_sem=send.at[n],
-            recv_sem=recv.at[n],
-            device_id={"space": peer},
-            device_id_type=MESH,
-        )
+        to_space(gap.at[peer], landed.at[me], x_send.at[n], x_recv.at[n], peer)
         for n, peer in enumerate(peers)
     ]
     for copy in copies:
         copy.start()
-    out[me] = blocks[me]
-    for n, copy in enumerate(copies):
+    for copy in fetches:
         copy.wait()
-        origin = lax.rem(me + size - 1 - n, size)
-        out[origin] = landed[origin]
-
-
-def exchange(blocks, size, number):
-    vmem = pl.BlockSpec(memory_space=pltpu.VMEM)
-    return pl.pallas_call(
-        functools.partial(exchange_kernel, size),
-        out_shape=jax.ShapeDtypeStruct(blocks.shape, jnp.float32),
-        in_specs=[vmem],
-        out_specs=vmem,
-        scratch_shapes=[pltpu.VMEM(blocks.shape, jnp.float32)]
-        + [pltpu.SemaphoreType.DMA((size - 1,))] * 2,
-        compiler_params=pltpu.CompilerParams(
-            collective_id=number, has_side_effects=True, vmem_limit_bytes=16 << 20
-        ),
-        cost_estimate=pl.CostEstimate(
-            flops=0, bytes_accessed=30 * blocks.size, transcendentals=0
-        ),
-    )(blocks)
-
-
-def apply_operator(s, wave_east, wave_north):
-    turn = lambda a: jnp.stack([a[:, 1], -a[:, 0]], 1)
-    h, u, v = s
-    return (
-        turn(wave_east * u + wave_north * v),
-        wave_east * turn(h) + CORIOLIS * v,
-        wave_north * turn(h) - CORIOLIS * u,
-    )
-
-
-def propagate(s, wave_east, wave_north, sine, versine):
-    once = apply_operator(s, wave_east, wave_north)
-    twice = apply_operator(once, wave_east, wave_north)
-    return jnp.stack([a + sine * b + versine * c for a, b, c in zip(s, once, twice)])
+
+    def y_spectra(block, at):
+        up, down = split(block)
+        return dot(up, ah[at]) + (dot(down, ah[at]) + dot(up, al[at]))
+
+    acc[...] = y_spectra(gap[me], me)
+    for copy, origin in zip(copies, origins):
+        copy.wait_recv()
+        acc[...] += y_spectra(landed[origin], origin)
+
+    def propagate(more):
+        for r in range(0, count, 8):
+            at = slice(r, r + 8)
+            state_of = []
+            for f in range(fields):
+                row = slice(f * count + r, f * count + r + 8)
+                pair = [acc[row, :nc], acc[row, nc:]]
+                if more is not None:
+                    extra = (relayed[more, row, :nc], relayed[more, row, nc:])
+                    pair = [p + jnp.where(slot == 0, 0.0, q) for p, q in zip(pair, extra)]
+                state_of.append(pair)
+            once = apply_operator(state_of, east[at], north[...])
+            twice = apply_operator(once, east[at], north[...])
+            for f in range(fields):
+                row = slice(f * count + r, f * count + r + 8)
+                for part, lanes in enumerate((slice(0, nc), slice(nc, 2 * nc))):
+                    change[row, lanes] = (
+                        state_of[f][part]
+                        + sine[at] * once[f][part]
+                        + versine[at] * twice[f][part]
+                    )
+
+    propagate(None)
+    for n in range(slices - 1):
+        ahead = to_next(change, relayed.at[n], 1 + n)
+        ahead.start()
+        ahead.wait()
+        propagate(n)
+
+    up, down = split(change[...])
+
+    def y_fields(at):
+        return dot(up, bh[at]) + (dot(down, bh[at]) + dot(up, bl[at]))
+
+    home = []
+    for n, peer in enumerate(peers):
+        leaving[peer] = y_fields(peer)
+        home.append(to_space(leaving.at[peer], returned.at[me], y_send.at[n], y_recv.at[n], peer))
+        home[-1].start()
+    out[me] = y_fields(me)
+    for copy in copies:
+        copy.wait_send()
+    for copy, origin in zip(home, origins):
+        copy.wait()
+        out[origin] = returned[origin]
 
 
 def shards(start_old, incoming):
     size, slices = lax.axis_size("space"), lax.axis_size("tm")
     state = start_old[0]
     width = state.shape[2]
-    rows, nc = incoming.shape[1:]
+    fields, rows, nc = incoming.shape
     half = nc // 2
     count = half // size
     forward, wide, along, back, inverse, wave, sine, versine = tables(nc, size)
     pairs = np.repeat(np.eye(rows, dtype=np.float32), RATIO, axis=1)
 
-    is_first = (lax.axis_index("tm") == 0).astype(jnp.float32)
-    start_rows = dot("yY,fYx->fyx", 0.5 * pairs, state)
-    drift = dot("ckx,fyx->ckfy", wide, start_rows)
-    drift = drift - dot("ckx,fyx->ckfy", forward, is_first * incoming)
-
     fine = heun(state, size)
-    coarse_rows = dot("yY,fYx->fyx", 0.5 * pairs, fine)
-    coarse = dot("ckx,fyx->ckfy", wide, coarse_rows)
-    route = [(i, i + 1) for i in range(slices - 1)]
-    gap = lax.ppermute(coarse, "tm", route) - drift
-
-    gap = gap.reshape(2, size, count, 3, rows).transpose(1, 3, 2, 0, 4)
-    gap = gap.reshape(size, 3 * count, 2 * rows)
-    piece = exchange(gap, size, 1)
-    spectra = split_dot("imy,iyq->mq", piece, along.reshape(size, 2 * rows, 2 * nc))
-    spectra = spectra.reshape(3, count, 2, nc)
-
-    mine = lax.axis_index("space") * count
-    cut = lambda a: lax.dynamic_slice_in_dim(jnp.asarray(a), mine, count, 0)
-    wave_east = cut(wave[:half])[:, None, None]
-    wave_north = wave[None, None, :]
-    factors = (wave_east, wave_north, cut(sine)[:, None, :], cut(versine)[:, None, :])
-    change = propagate(spectra, *factors)
-    for _ in range(slices - 1):
-        change = propagate(spectra + lax.ppermute(change, "tm", route), *factors)
-
-    change = change.reshape(3 * count, 2 * nc)
-    moved = split_dot("mq,qiy->imy", change, back.reshape(2 * nc, size, 2 * rows))
-    moved = exchange(moved, size, 2)
-    moved = moved.reshape(size, 3, count, 2, rows).transpose(1, 4, 3, 0, 2)
-    moved = moved.reshape(3, rows, nc)
-    moved = dot("yY,fyk->fYk", pairs, moved)
-    result = fine + dot("fYk,kx->fYx", moved, inverse.reshape(nc, width))
+
+    first = lax.axis_index("space") * count
+    cut = lambda a: lax.dynamic_slice_in_dim(jnp.asarray(a), first, count, 0)
+    flat = lambda table: halves(table.reshape(nc, -1))
+    back = back.reshape(2 * nc, size, 2 * rows).transpose(1, 0, 2)
+    east = np.repeat(wave[:half, None], nc, axis=1)
+    north = np.repeat(wave[None, :], 8, axis=0)
+    operands = [fine, state, incoming, (0.5 * pairs).astype(jnp.bfloat16)]
+    operands += [*flat(wide), *flat(forward), cut(east), north, cut(sine), cut(versine)]
+    distant = [*halves(along.reshape(size, 2 * rows, 2 * nc)), *halves(back)]
+    blocks = (size, fields * count, 2 * rows)
+    whole = (fields * count, 2 * nc)
+    shapes = [blocks] * 4 + [whole] * 2 + [(max(slices - 1, 1), *whole)] + [blocks] * 2
+    vmem = pl.BlockSpec(memory_space=pltpu.VMEM)
+    far = pl.BlockSpec(memory_space=pl.ANY)
+    moved = pl.pallas_call(
+        functools.partial(coarse_kernel, size, slices),
+        out_shape=jax.ShapeDtypeStruct(blocks, jnp.float32),
+        in_specs=[vmem] * len(operands) + [far] * len(distant),
+        out_specs=vmem,
+        scratch_shapes=[pltpu.VMEM(shape, jnp.float32) for shape in shapes]
+        + [pltpu.VMEM(table.shape, jnp.bfloat16) for table in distant]
+        + [pltpu.SemaphoreType.DMA((4,))]
+        + [pltpu.SemaphoreType.DMA((size - 1,))] * 4
+        + [pltpu.SemaphoreType.DMA((slices,))] * 2,
+        compiler_params=pltpu.CompilerParams(
+            collective_id=1, has_side_effects=True, vmem_limit_bytes=44 << 20
+        ),
+        cost_estimate=pl.CostEstimate(
+            flops=40 * fields * count * nc * nc, bytes_accessed=32 * nc * nc, transcendentals=0
+        ),
+    )(*operands, *distant)
+
+    moved = moved.reshape(size, fields, count, 2, rows).transpose(1, 4, 3, 0, 2)
+    moved = moved.reshape(fields, rows, nc)
+    matmul = functools.partial(
+        jnp.einsum, precision=lax.Precision.HIGH, preferred_element_type=jnp.float32
+    )
+    moved = matmul("yY,fyk->fYk", pairs, moved)
+    result = fine + matmul("fYk,kx->fYx", moved, inverse.reshape(nc, width))
     return result[None]
 
 

time: 70.3 us -> 58.3 us (0.83)
  matrix products: 14.7 us -> 3.27 us
  Pallas kernels: 39.1 us -> 45.9 us
  other arithmetic: 3.6 us -> 0 us
  starting transfers between devices: 3.54 us -> 0 us
  local copies, waits for them, and re-layouts: 7.26 us -> 8.58 us
  waiting for transfers between devices: 0.79 us -> 0 us
    dot_general x13 -> x2, matrix products: 14.7 us -> 3.27 us  [the longest x1 2.76 us: shards(): result = fine + matmul('fYk,kx->fYx', moved, inverse.reshape(nc, width))]
    pallas_call x2 -> x1, Pallas kernels: 22.3 us -> 29.3 us  [shards(): pl.pallas_call(functools.partial(coarse_kernel, size, slices), out_shape=...]
    ppermute x2 -> x0, starting transfers between devices: 3.54 us -> none  [the longest x1 2.05 us: shards(): gap = lax.ppermute(coarse, 'tm', route) - drift]
    unnamed x23 -> x24, local copies, waits for them, and re-layouts: 3.38 us -> 6.25 us
    add x6 -> x0, other arithmetic: 2.45 us -> none  [the longest x3 1.62 us: propagate(): a + sine * b + versine * c]
    another operation x5 -> x0, other arithmetic: 0.85 us -> none  [the longest x3 0.48 us: apply_operator(): turn = lambda a: jnp.stack([a[:, 1], -a[:, 0]], 1)]
    ppermute x2 -> x0, waiting for transfers between devices: 0.79 us -> none  [the longest x1 0.79 us: shards(): change = propagate(spectra + lax.ppermute(change, 'tm', route), *factors)]
    dynamic_slice x2, local copies, waits for them, and re-layouts: 0.99 us -> 1.78 us  [shards(): cut = lambda a: lax.dynamic_slice_in_dim(jnp.asarray(a), first, count, 0)]
  transfers between devices with their start and end apart: 2 -> 0, of which waited for: 1 -> 0; matrix products, arithmetic and copies ran while one was open for 7% -> 0% of each run, Pallas kernels for 0% -> 0%
where the time goes in v3:
time: 58.3 us; the launch traced here: 57.9 us
  Pallas kernels  45.9 us (79%)
  local copies, waits for them, and re-layouts  8.58 us (15%)
  matrix products  3.27 us (6%)
    pallas_call x1, Pallas kernels, shards(): pl.pallas_call(functools.partial(coarse_kernel, size, slices), out_shape=...  29.3 us
    pallas_call x1, Pallas kernels, heun(): pl.pallas_call(functools.partial(heun_kernel, size), out_shape=jax.ShapeD...  16.7 us
    unnamed x24, local copies, waits for them, and re-layouts  6.25 us
    dot_general x1, matrix products, shards(): result = fine + matmul('fYk,kx->fYx', moved, inverse.reshape(nc, width))  2.76 us
    dynamic_slice x2, local copies, waits for them, and re-layouts, shards(): cut = lambda a: lax.dynamic_slice_in_dim(jnp.asarray(a), first, count, 0)  1.78 us

profile of v3, /device:TPU:0, one launch (start us, length us, event | category | flops | bytes accessed | tf_op | source)
XLA Modules:
  0.0 57.9 jit_solution(14968031002486822948)
XLA Ops:
  0.0 0.0 copy-start.8
  0.0 0.0 copy-start.9
  0.0 0.0 copy-start.7
  0.0 0.9 %constant_dynamic-slice_fusion.2.east = f32[32,512]{1,0:T(8,128)S(1)} fusion(f32[256,512]{1,0:T(8,128)} %constant.40.clone, s32[]{:T(128)S(6)} %select_n.2), kind=kLoop, calls=%fused_computation.4 | loop fusion | bytes 131076 | tf_op jit(solution)/shard_map/dynamic_slice | solution.py:343
  0.9 0.9 %constant_dynamic-slice_fusion = (f32[32,512]{1,0:T(8,128)S(1)}, f32[32,512]{1,0:T(8,128)S(1)}) fusion(f32[256,512]{1,0:T(8,128)} %constant.42.clone, s32[]{:T(128)S(6)} %select_n.2, f32[256,512]{1,0:T(8,128)} %constant.41.clone), kind=kLoop, calls=%fused_computation.2 | loop fusion | bytes 262148 | tf_op jit(solution)/shard_map/dynamic_slice | solution.py:343
  1.8 0.0 copy-start
  1.8 1.4 %copy-done = f32[1,3,128,1024]{3,2,1,0:T(8,128)S(1)} copy-done((f32[1,3,128,1024]{3,2,1,0:T(8,128)S(1)}, f32[1,3,128,1024]{3,2,1,0:T(8,128)}, u32[]{:S(2)}) %copy-start) | copy-done | bytes 1572888
  3.2 0.0 copy-start.1
  3.2 0.0 copy-start.3
  3.2 0.0 copy-start.5
  3.2 16.7 %shard_map.163.fine = f32[3,128,1024]{2,1,0:T(8,128)S(1)} custom-call(f32[3,128,1024]{2,1,0:T(8,128)S(1)} %bitcast.14), custom_call_target="tpu_custom_call" | custom-call | flops 26214400 | bytes 3145728 | tf_op jit(solution)/shard_map/pallas_call | solution.py:166
  19.9 0.0 copy-done.8
  19.9 0.0 copy-done.9
  19.9 0.0 copy-done.7
  19.9 0.0 copy-done.1
  19.9 0.0 copy-done.3
  19.9 0.0 copy-done.5
  19.9 0.0 copy-start.2
  19.9 1.6 %copy-done.2 = bf16[8,128,1024]{2,1,0:T(8,128)(2,1)S(1)} copy-done((bf16[8,128,1024]{2,1,0:T(8,128)(2,1)S(1)}, bf16[8,128,1024]{2,1,0:T(8,128)(2,1)}, u32[]{:S(2)}) %copy-start.2) | copy-done | bytes 2097176
  21.5 0.0 copy-start.4
  21.5 1.2 %copy-done.4 = bf16[512,1024]{1,0:T(8,128)(2,1)S(1)} copy-done((bf16[512,1024]{1,0:T(8,128)(2,1)S(1)}, bf16[512,1024]{1,0:T(8,128)(2,1)}, u32[]{:S(2)}) %copy-start.4) | copy-done | bytes 1048600
  22.8 0.0 copy-start.6
  22.8 1.0 %copy-done.6 = bf16[512,512]{1,0:T(8,128)(2,1)S(1)} copy-done((bf16[512,512]{1,0:T(8,128)(2,1)S(1)}, bf16[512,512]{1,0:T(8,128)(2,1)}, u32[]{:S(2)}) %copy-start.6) | copy-done | bytes 524312
  23.8 29.3 %shard_map.164 = f32[8,96,128]{2,1,0:T(8,128)S(1)} custom-call(f32[3,128,1024]{2,1,0:T(8,128)S(1)} %shard_map.163.fine, f32[3,128,1024]{2,1,0:T(8,128)S(1)} %bitcast.15, f32[3,64,512]{2,1,0:T(8,128)S(1)} %copy-done.7, bf16[64,128]{1,0:T(8,128)(2,1)S(1)} %copy-done.9, bf16[512,1024]{1,0:T(8,128)(2,1)S(1)} %copy-done.4, bf16[512,1024]{1,0:T(8,128)(2,1)S(1)} %copy-done.3, ...), custom_call_target="tpu_custom_call" | custom-call | flops 1006632960 | bytes 8388608 | tf_op jit(solution)/shard_map/pallas_call | solution.py:356
  53.1 0.0 copy-start.11
  53.1 0.5 reshape.6
  53.6 0.0 copy-start.10
  53.6 0.1 copy.18
  53.7 0.2 copy-done.11
  53.8 0.5 convolution_bitcast_fusion
  54.4 0.8 %copy-done.10 = f32[512,1024,1]{1,0,2:T(8,128)S(1)} copy-done((f32[512,1024,1]{1,0,2:T(8,128)S(1)}, f32[512,1024,1]{1,0,2:T(8,128)}, u32[]{:S(2)}) %copy-start.10) | copy-done | bytes 2097176
  55.2 2.8 %add_bitcast_fusion = f32[1,3,128,1024]{3,2,1,0:T(8,128)} fusion(f32[3,128,1024]{2,1,0:T(8,128)S(1)} %shard_map.163.fine, f32[3,128,512]{2,1,0:T(8,128)S(1)} %convolution_bitcast_fusion, f32[512,1024,1]{1,0,2:T(8,128)S(1)} %copy-done.10), kind=kOutput, calls=%fused_computation | convolution fusion | flops 1208352768 | bytes 6029312 | tf_op jit(solution)/shard_map/fYk,kx->fYx/dot_general | solution.py:380
Async XLA Ops:
  0.0 19.9 %copy-start.8 = (f32[8,512]{1,0:T(8,128)S(1)}, f32[8,512]{1,0:T(8,128)}, u32[]{:S(2)}) copy-start(f32[8,512]{1,0:T(8,128)} %constant.48.clone.north) | copy-start | bytes 49156
  0.0 19.9 %copy-start.9 = (bf16[64,128]{1,0:T(8,128)(2,1)S(1)}, bf16[64,128]{1,0:T(8,128)(2,1)}, u32[]{:S(2)}) copy-start(bf16[64,128]{1,0:T(8,128)(2,1)} %constant.43.clone.pairs) | copy-start | bytes 49156
  0.0 19.9 %copy-start.7 = (f32[3,64,512]{2,1,0:T(8,128)S(1)}, f32[3,64,512]{2,1,0:T(8,128)}, u32[]{:S(2)}) copy-start(f32[3,64,512]{2,1,0:T(8,128)} %incoming.1) | copy-start | bytes 1179652
  1.8 1.4 %copy-start = (f32[1,3,128,1024]{3,2,1,0:T(8,128)S(1)}, f32[1,3,128,1024]{3,2,1,0:T(8,128)}, u32[]{:S(2)}) copy-start(f32[1,3,128,1024]{3,2,1,0:T(8,128)} %param.17) | copy-start | bytes 4718596
  3.2 16.7 %copy-start.1 = (f32[1,3,128,1024]{3,2,1,0:T(8,128)S(1)}, f32[1,3,128,1024]{3,2,1,0:T(8,128)}, u32[]{:S(2)}) copy-start(f32[1,3,128,1024]{3,2,1,0:T(8,128)} %param.17) | copy-start | bytes 4718596
  3.2 16.7 %copy-start.3 = (bf16[512,1024]{1,0:T(8,128)(2,1)S(1)}, bf16[512,1024]{1,0:T(8,128)(2,1)}, u32[]{:S(2)}) copy-start(bf16[512,1024]{1,0:T(8,128)(2,1)} %constant.45.clone.wide_l) | copy-start | bytes 3145732
  3.2 16.7 %copy-start.5 = (bf16[512,512]{1,0:T(8,128)(2,1)S(1)}, bf16[512,512]{1,0:T(8,128)(2,1)}, u32[]{:S(2)}) copy-start(bf16[512,512]{1,0:T(8,128)(2,1)} %constant.47.clone.short_l) | copy-start | bytes 1572868
  19.9 1.6 %copy-start.2 = (bf16[8,128,1024]{2,1,0:T(8,128)(2,1)S(1)}, bf16[8,128,1024]{2,1,0:T(8,128)(2,1)}, u32[]{:S(2)}) copy-start(bf16[8,128,1024]{2,1,0:T(8,128)(2,1)} %constant.49.clone.along_h) | copy-start | bytes 6291460
  21.5 1.2 %copy-start.4 = (bf16[512,1024]{1,0:T(8,128)(2,1)S(1)}, bf16[512,1024]{1,0:T(8,128)(2,1)}, u32[]{:S(2)}) copy-start(bf16[512,1024]{1,0:T(8,128)(2,1)} %constant.44.clone.wide_h) | copy-start | bytes 3145732
  22.8 1.0 %copy-start.6 = (bf16[512,512]{1,0:T(8,128)(2,1)S(1)}, bf16[512,512]{1,0:T(8,128)(2,1)}, u32[]{:S(2)}) copy-start(bf16[512,512]{1,0:T(8,128)(2,1)} %constant.46.clone.short_h) | copy-start | bytes 1572868
  53.1 0.8 %copy-start.11 = (f32[64,128,1]{1,0,2:T(8,128)S(1)}, f32[64,128,1]{1,0,2:T(8,128)}, u32[]{:S(2)}) copy-start(f32[64,128,1]{1,0,2:T(8,128)} %constant.57) | copy-start | bytes 98308
  53.6 1.6 %copy-start.10 = (f32[512,1024,1]{1,0,2:T(8,128)S(1)}, f32[512,1024,1]{1,0,2:T(8,128)}, u32[]{:S(2)}) copy-start(f32[512,1024,1]{1,0,2:T(8,128)} %constant.58) | copy-start | bytes 6291460

commit v4 on v3

--- a/solution.py
+++ b/solution.py
@@ -87,34 +87,9 @@
     return row if isinstance(row, int) else pl.multiple_of(row, 8)
 
 
-def greet(peers):
-    barrier = pltpu.get_barrier_semaphore()
-    for peer in peers:
-        pl.semaphore_signal(barrier, inc=1, device_id={"space": peer}, device_id_type=MESH)
-    pl.semaphore_wait(barrier, len(peers))
-
-
-def heun_kernel(size, state, fine, now, first, send, recv):
+def heun(state, fine, now, first, exchange_rims):
     rows = state.shape[1]
     blocks = (rows + 2 * HALO) // 8
-    me = lax.axis_index("space")
-    after, before = lax.rem(me + 1, size), lax.rem(me + size - 1, size)
-    greet((after, before))
-    copies = [
-        pltpu.make_async_remote_copy(
-            src_ref=state.at[:, pl.ds(source, HALO)],
-            dst_ref=now.at[:, pl.ds(target, HALO)],
-            send_sem=send.at[n],
-            recv_sem=recv.at[n],
-            device_id={"space": peer},
-            device_id_type=MESH,
-        )
-        for n, (source, target, peer) in enumerate(
-            ((rows - HALO, 8, after), (0, 16 + rows, before))
-        )
-    ]
-    for copy in copies:
-        copy.start()
     pad = jnp.zeros((HALO, state.shape[2]), jnp.float32)
     for f in range(3):
         now[f, 16 : 16 + rows] = state[f]
@@ -147,8 +122,7 @@
     for step in range(STEPS):
         if step == 0:
             lax.fori_loop(2, blocks - 2, predict, 0)
-            for copy in copies:
-                copy.wait()
+            exchange_rims()
             for block in (0, 1, blocks - 2, blocks - 1):
                 predict(block, 0)
         else:
@@ -159,25 +133,6 @@
             lax.fori_loop(1, blocks - 1, correct(fine, 16), 0)
 
 
-def heun(state, size):
-    fields, rows, width = state.shape
-    vmem = pl.BlockSpec(memory_space=pltpu.VMEM)
-    padded = pltpu.VMEM((fields, rows + 4 * HALO, width), jnp.float32)
-    return pl.pallas_call(
-        functools.partial(heun_kernel, size),
-        out_shape=jax.ShapeDtypeStruct(state.shape, jnp.float32),
-        in_specs=[vmem],
-        out_specs=vmem,
-        scratch_shapes=[padded, padded] + [pltpu.SemaphoreType.DMA((2,))] * 2,
-        compiler_params=pltpu.CompilerParams(
-            collective_id=0, has_side_effects=True, vmem_limit_bytes=8 << 20
-        ),
-        cost_estimate=pl.CostEstimate(
-            flops=200 * rows * width, bytes_accessed=24 * rows * width, transcendentals=0
-        ),
-    )(state)
-
-
 def apply_operator(s, a, b):
     (hr, hi), (ur, ui), (vr, vi) = s
     return (
@@ -187,11 +142,13 @@
     )
 
 
-def coarse_kernel(
-    size, slices, fine, state, incoming, pairs, wide_h, wide_l, short_h, short_l,
-    east, north, sine, versine, along_h, along_l, back_h, back_l, out,
-    mine, theirs, gap, landed, acc, change, relayed, leaving, returned,
-    ah, al, bh, bl, fetch, x_send, x_recv, y_send, y_recv, t_send, t_recv,
+def kernel(
+    size, slices, state, incoming, pairs, north,
+    wide_h_far, wide_l_far, short_h_far, short_l_far, along_h, along_l, back_h, back_l,
+    east_far, sine_far, versine_far, fine, out,
+    now, first, mine, theirs, gap, landed, acc, change, relayed, leaving, returned,
+    east, sine, versine, wide_h, wide_l, short_h, short_l, ah, al, bh, bl,
+    fetch, x_send, x_recv, y_send, y_recv, t_send, t_recv, rim_send, rim_recv,
 ):
     fields, rows, nc = incoming.shape
     half = nc // 2
@@ -201,10 +158,23 @@
     origins = [lax.rem(me + size - d, size) for d in range(1, size)]
     following, previous = lax.rem(slot + 1, slices), lax.rem(slot + slices - 1, slices)
 
+    share = pl.ds(pl.multiple_of(me * count, count), count)
     fetches = [
         pltpu.make_async_copy(source, target, fetch.at[n])
         for n, (source, target) in enumerate(
-            ((along_h, ah), (along_l, al), (back_h, bh), (back_l, bl))
+            (
+                (wide_h_far, wide_h),
+                (wide_l_far, wide_l),
+                (short_h_far, short_h),
+                (short_l_far, short_l),
+                (along_h, ah),
+                (along_l, al),
+                (east_far.at[share], east),
+                (sine_far.at[share], sine),
+                (versine_far.at[share], versine),
+                (back_h, bh),
+                (back_l, bl),
+            )
         )
     ]
     for copy in fetches:
@@ -250,26 +220,57 @@
     def put_gap(j, at, value):
         gap[j, at] = value
 
-    lay_out(x_spectra(fine), put_mine)
-    pl.semaphore_wait(barrier, len(peers) + 2)
-    ahead = to_next(mine, theirs, 0)
-    ahead.start()
-    fresh = jnp.concatenate([incoming[f] for f in range(fields)], 0)
-    fresh = spectra_of(fresh, short_h[...], short_l[...])
-    drift = x_spectra(state) - jnp.where(slot == 0, fresh, 0.0)
-    lay_out(-drift, put_gap)
-    ahead.wait()
-    for j in range(size):
-        gap[j] = gap[j] + jnp.where(slot == 0, 0.0, theirs[j])
-
     copies = [
         to_space(gap.at[peer], landed.at[me], x_send.at[n], x_recv.at[n], peer)
         for n, peer in enumerate(peers)
     ]
-    for copy in copies:
-        copy.start()
-    for copy in fetches:
+    wide_rows = state.shape[1]
+    rims = [
+        to_space(
+            state.at[:, pl.ds(source, HALO)], now.at[:, pl.ds(target, HALO)],
+            rim_send.at[n], rim_recv.at[n], peer,
+        )
+        for n, (source, target, peer) in enumerate(
+            ((wide_rows - HALO, 8, peers[0]), (0, 16 + wide_rows, peers[-1]))
+        )
+    ]
+
+    def exchange_rims():
+        pl.semaphore_wait(barrier, len(peers) + 2)
+        for copy in rims:
+            copy.start()
+        for copy in fetches[:4]:
+            copy.wait()
+        fresh = jnp.concatenate([incoming[f] for f in range(fields)], 0)
+        fresh = spectra_of(fresh, short_h[...], short_l[...])
+        drift = x_spectra(state) - jnp.where(slot == 0, fresh, 0.0)
+        lay_out(-drift, put_gap)
+        for copy in rims:
+            copy.wait()
+
+        @pl.when(slot == 0)
+        def _():
+            for copy in copies:
+                copy.start()
+
+    heun(state, fine, now, first, exchange_rims)
+    lay_out(x_spectra(fine), put_mine)
+    ahead = to_next(mine, theirs, 0)
+
+    @pl.when(slot < slices - 1)
+    def _():
+        ahead.start()
+
+    for copy in fetches[4:]:
         copy.wait()
+
+    @pl.when(slot > 0)
+    def _():
+        ahead.wait_recv()
+        for j in range(size):
+            gap[j] = gap[j] + theirs[j]
+        for copy in copies:
+            copy.start()
 
     def y_spectra(block, at):
         up, down = split(block)
@@ -280,34 +281,28 @@
         copy.wait_recv()
         acc[...] += y_spectra(landed[origin], origin)
 
-    def propagate(more):
-        for r in range(0, count, 8):
-            at = slice(r, r + 8)
-            state_of = []
-            for f in range(fields):
-                row = slice(f * count + r, f * count + r + 8)
-                pair = [acc[row, :nc], acc[row, nc:]]
-                if more is not None:
-                    extra = (relayed[more, row, :nc], relayed[more, row, nc:])
-                    pair = [p + jnp.where(slot == 0, 0.0, q) for p, q in zip(pair, extra)]
-                state_of.append(pair)
-            once = apply_operator(state_of, east[at], north[...])
-            twice = apply_operator(once, east[at], north[...])
-            for f in range(fields):
-                row = slice(f * count + r, f * count + r + 8)
-                for part, lanes in enumerate((slice(0, nc), slice(nc, 2 * nc))):
-                    change[row, lanes] = (
-                        state_of[f][part]
-                        + sine[at] * once[f][part]
-                        + versine[at] * twice[f][part]
-                    )
-
-    propagate(None)
-    for n in range(slices - 1):
-        ahead = to_next(change, relayed.at[n], 1 + n)
-        ahead.start()
-        ahead.wait()
-        propagate(n)
+    relay = to_next(change, relayed, 1)
+
+    @pl.when(slot > 0)
+    def _():
+        relay.wait_recv()
+        acc[...] += relayed[...]
+
+    for r in range(0, count, 8):
+        at = slice(r, r + 8)
+        places = [slice(f * count + r, f * count + r + 8) for f in range(fields)]
+        spectra = [(acc[row, :nc], acc[row, nc:]) for row in places]
+        once = apply_operator(spectra, east[at], north[...])
+        twice = apply_operator(once, east[at], north[...])
+        for f, row in enumerate(places):
+            for part, lanes in enumerate((slice(0, nc), slice(nc, 2 * nc))):
+                change[row, lanes] = (
+                    spectra[f][part] + sine[at] * once[f][part] + versine[at] * twice[f][part]
+                )
+
+    @pl.when(slot < slices - 1)
+    def _():
+        relay.start()
 
     up, down = split(change[...])
 
@@ -322,6 +317,12 @@
     out[me] = y_fields(me)
     for copy in copies:
         copy.wait_send()
+
+    @pl.when(slot < slices - 1)
+    def _():
+        ahead.wait_send()
+        relay.wait_send()
+
     for copy, origin in zip(home, origins):
         copy.wait()
         out[origin] = returned[origin]
@@ -337,39 +338,36 @@
     forward, wide, along, back, inverse, wave, sine, versine = tables(nc, size)
     pairs = np.repeat(np.eye(rows, dtype=np.float32), RATIO, axis=1)
 
-    fine = heun(state, size)
-
-    first = lax.axis_index("space") * count
-    cut = lambda a: lax.dynamic_slice_in_dim(jnp.asarray(a), first, count, 0)
     flat = lambda table: halves(table.reshape(nc, -1))
     back = back.reshape(2 * nc, size, 2 * rows).transpose(1, 0, 2)
     east = np.repeat(wave[:half, None], nc, axis=1)
     north = np.repeat(wave[None, :], 8, axis=0)
-    operands = [fine, state, incoming, (0.5 * pairs).astype(jnp.bfloat16)]
-    operands += [*flat(wide), *flat(forward), cut(east), north, cut(sine), cut(versine)]
-    distant = [*halves(along.reshape(size, 2 * rows, 2 * nc)), *halves(back)]
+    operands = [state, incoming, (0.5 * pairs).astype(jnp.bfloat16), north]
+    distant = [*flat(wide), *flat(forward)]
+    distant += [*halves(along.reshape(size, 2 * rows, 2 * nc)), *halves(back)]
     blocks = (size, fields * count, 2 * rows)
     whole = (fields * count, 2 * nc)
-    shapes = [blocks] * 4 + [whole] * 2 + [(max(slices - 1, 1), *whole)] + [blocks] * 2
+    padded = (fields, state.shape[1] + 4 * HALO, width)
+    shapes = [padded] * 2 + [blocks] * 4 + [whole] * 3 + [blocks] * 2 + [(count, nc)] * 3
     vmem = pl.BlockSpec(memory_space=pltpu.VMEM)
     far = pl.BlockSpec(memory_space=pl.ANY)
-    moved = pl.pallas_call(
-        functools.partial(coarse_kernel, size, slices),
-        out_shape=jax.ShapeDtypeStruct(blocks, jnp.float32),
-        in_specs=[vmem] * len(operands) + [far] * len(distant),
-        out_specs=vmem,
+    fine, moved = pl.pallas_call(
+        functools.partial(kernel, size, slices),
+        out_shape=[jax.ShapeDtypeStruct(shape, jnp.float32) for shape in (state.shape, blocks)],
+        in_specs=[vmem] * len(operands) + [far] * (len(distant) + 3),
+        out_specs=[vmem] * 2,
         scratch_shapes=[pltpu.VMEM(shape, jnp.float32) for shape in shapes]
         + [pltpu.VMEM(table.shape, jnp.bfloat16) for table in distant]
-        + [pltpu.SemaphoreType.DMA((4,))]
+        + [pltpu.SemaphoreType.DMA((len(distant) + 3,))]
         + [pltpu.SemaphoreType.DMA((size - 1,))] * 4
-        + [pltpu.SemaphoreType.DMA((slices,))] * 2,
+        + [pltpu.SemaphoreType.DMA((2,))] * 4,
         compiler_params=pltpu.CompilerParams(
-            collective_id=1, has_side_effects=True, vmem_limit_bytes=44 << 20
+            collective_id=0, has_side_effects=True, vmem_limit_bytes=48 << 20
         ),
         cost_estimate=pl.CostEstimate(
             flops=40 * fields * count * nc * nc, bytes_accessed=32 * nc * nc, transcendentals=0
         ),
-    )(*operands, *distant)
+    )(*operands, *distant, east, sine, versine)
 
     moved = moved.reshape(size, fields, count, 2, rows).transpose(1, 4, 3, 0, 2)
     moved = moved.reshape(fields, rows, nc)

time: 58.3 us -> 55.9 us (0.959)
  the two profiles are of different devices: /device:TPU:0 before, /device:TPU:1 now
where the time goes in v4:
time: 55.9 us; the launch traced here: 55.3 us
  Pallas kernels  40.3 us (72%)
  local copies, waits for them, and re-layouts  11.7 us (21%)
  matrix products  3.24 us (6%)
    pallas_call x1, Pallas kernels, shards(): pl.pallas_call(functools.partial(kernel, size, slices), out_shape=[jax.Sh...  40.3 us
    unnamed x26, local copies, waits for them, and re-layouts  11.1 us
    dot_general x1, matrix products, shards(): result = fine + matmul('fYk,kx->fYx', moved, inverse.reshape(nc, width))  2.72 us

profile of v4, /device:TPU:1, one launch (start us, length us, event | category | flops | bytes accessed | tf_op | source)
XLA Modules:
  0.0 55.3 jit_solution(6454458605353878972)
XLA Ops:
  0.0 0.0 copy-start
  0.0 1.2 %copy-done = bf16[512,1024]{1,0:T(8,128)(2,1)S(1)} copy-done((bf16[512,1024]{1,0:T(8,128)(2,1)S(1)}, bf16[512,1024]{1,0:T(8,128)(2,1)}, u32[]{:S(2)}) %copy-start) | copy-done | bytes 1048600
  1.2 0.0 copy-start.1
  1.2 1.2 %copy-done.1 = bf16[512,1024]{1,0:T(8,128)(2,1)S(1)} copy-done((bf16[512,1024]{1,0:T(8,128)(2,1)S(1)}, bf16[512,1024]{1,0:T(8,128)(2,1)}, u32[]{:S(2)}) %copy-start.1) | copy-done | bytes 1048600
  2.5 0.0 copy-start.2
  2.5 1.0 %copy-done.2 = f32[256,512]{1,0:T(8,128)S(1)} copy-done((f32[256,512]{1,0:T(8,128)S(1)}, f32[256,512]{1,0:T(8,128)}, u32[]{:S(2)}) %copy-start.2) | copy-done | bytes 524312
  3.5 0.0 copy-start.3
  3.5 1.0 %copy-done.3 = f32[256,512]{1,0:T(8,128)S(1)} copy-done((f32[256,512]{1,0:T(8,128)S(1)}, f32[256,512]{1,0:T(8,128)}, u32[]{:S(2)}) %copy-start.3) | copy-done | bytes 524312
  4.5 0.0 copy-start.4
  4.5 1.0 %copy-done.4 = f32[256,512]{1,0:T(8,128)S(1)} copy-done((f32[256,512]{1,0:T(8,128)S(1)}, f32[256,512]{1,0:T(8,128)}, u32[]{:S(2)}) %copy-start.4) | copy-done | bytes 524312
  5.6 0.0 copy-start.5
  5.6 1.0 %copy-done.5 = bf16[512,512]{1,0:T(8,128)(2,1)S(1)} copy-done((bf16[512,512]{1,0:T(8,128)(2,1)S(1)}, bf16[512,512]{1,0:T(8,128)(2,1)}, u32[]{:S(2)}) %copy-start.5) | copy-done | bytes 524312
  6.6 0.0 copy-start.6
  6.6 1.0 %copy-done.6 = bf16[512,512]{1,0:T(8,128)(2,1)S(1)} copy-done((bf16[512,512]{1,0:T(8,128)(2,1)S(1)}, bf16[512,512]{1,0:T(8,128)(2,1)}, u32[]{:S(2)}) %copy-start.6) | copy-done | bytes 524312
  7.7 0.0 copy-start.7
  7.7 1.0 %copy-done.7 = f32[3,64,512]{2,1,0:T(8,128)S(1)} copy-done((f32[3,64,512]{2,1,0:T(8,128)S(1)}, f32[3,64,512]{2,1,0:T(8,128)}, u32[]{:S(2)}) %copy-start.7) | copy-done | bytes 393240
  8.7 0.0 copy-start.8
  8.7 0.7 %copy-done.8 = f32[8,512]{1,0:T(8,128)S(1)} copy-done((f32[8,512]{1,0:T(8,128)S(1)}, f32[8,512]{1,0:T(8,128)}, u32[]{:S(2)}) %copy-start.8) | copy-done | bytes 16408
  9.4 0.0 copy-start.9
  9.4 0.7 %copy-done.9 = bf16[64,128]{1,0:T(8,128)(2,1)S(1)} copy-done((bf16[64,128]{1,0:T(8,128)(2,1)S(1)}, bf16[64,128]{1,0:T(8,128)(2,1)}, u32[]{:S(2)}) %copy-start.9) | copy-done | bytes 16408
  10.1 40.3 %shard_map.163 = (f32[3,128,1024]{2,1,0:T(8,128)}, f32[8,96,128]{2,1,0:T(8,128)S(1)}) custom-call(f32[3,128,1024]{2,1,0:T(8,128)} %bitcast.15, f32[3,64,512]{2,1,0:T(8,128)S(1)} %copy-done.7, bf16[64,128]{1,0:T(8,128)(2,1)S(1)} %copy-done.9, f32[8,512]{1,0:T(8,128)S(1)} %copy-done.8, bf16[512,1024]{1,0:T(8,128)(2,1)S(1)} %copy-done.1, ...), custom_call_target="tpu_custom_call" | custom-call | flops 1006632960 | bytes 8388608 | tf_op jit(solution)/shard_map/pallas_call | solution.py:354
  50.4 0.0 copy-start.12
  50.4 0.0 copy-start.10
  50.4 0.5 reshape.6
  50.9 0.0 copy-start.11
  50.9 0.1 copy.18
  51.0 0.2 copy-done.12
  51.1 0.5 convolution_bitcast_fusion
  51.7 0.3 copy-done.10
  52.0 0.6 %copy-done.11 = f32[3,128,1024]{2,1,0:T(8,128)S(1)} copy-done((f32[3,128,1024]{2,1,0:T(8,128)S(1)}, f32[3,128,1024]{2,1,0:T(8,128)}, u32[]{:S(2)}) %copy-start.11) | copy-done | bytes 1572888
  52.5 2.7 %add_bitcast_fusion = f32[1,3,128,1024]{3,2,1,0:T(8,128)} fusion(f32[3,128,1024]{2,1,0:T(8,128)S(1)} %copy-done.11, f32[3,128,512]{2,1,0:T(8,128)S(1)} %convolution_bitcast_fusion, f32[512,1024,1]{1,0,2:T(8,128)S(1)} %copy-done.10), kind=kOutput, calls=%fused_computation | convolution fusion | flops 1208352768 | bytes 6029312 | tf_op jit(solution)/shard_map/fYk,kx->fYx/dot_general | solution.py:378
Async XLA Ops:
  0.0 1.2 %copy-start = (bf16[512,1024]{1,0:T(8,128)(2,1)S(1)}, bf16[512,1024]{1,0:T(8,128)(2,1)}, u32[]{:S(2)}) copy-start(bf16[512,1024]{1,0:T(8,128)(2,1)} %constant.33.clone.wide_l_far) | copy-start | bytes 3145732
  1.2 1.2 %copy-start.1 = (bf16[512,1024]{1,0:T(8,128)(2,1)S(1)}, bf16[512,1024]{1,0:T(8,128)(2,1)}, u32[]{:S(2)}) copy-start(bf16[512,1024]{1,0:T(8,128)(2,1)} %constant.32.clone.wide_h_far) | copy-start | bytes 3145732
  2.5 1.0 %copy-start.2 = (f32[256,512]{1,0:T(8,128)S(1)}, f32[256,512]{1,0:T(8,128)}, u32[]{:S(2)}) copy-start(f32[256,512]{1,0:T(8,128)} %constant.42.clone.versine_far) | copy-start | bytes 1572868
  3.5 1.0 %copy-start.3 = (f32[256,512]{1,0:T(8,128)S(1)}, f32[256,512]{1,0:T(8,128)}, u32[]{:S(2)}) copy-start(f32[256,512]{1,0:T(8,128)} %constant.41.clone.sine_far) | copy-start | bytes 1572868
  4.5 1.0 %copy-start.4 = (f32[256,512]{1,0:T(8,128)S(1)}, f32[256,512]{1,0:T(8,128)}, u32[]{:S(2)}) copy-start(f32[256,512]{1,0:T(8,128)} %constant.40.clone.east_far) | copy-start | bytes 1572868
  5.6 1.0 %copy-start.5 = (bf16[512,512]{1,0:T(8,128)(2,1)S(1)}, bf16[512,512]{1,0:T(8,128)(2,1)}, u32[]{:S(2)}) copy-start(bf16[512,512]{1,0:T(8,128)(2,1)} %constant.35.clone.short_l_far) | copy-start | bytes 1572868
  6.6 1.0 %copy-start.6 = (bf16[512,512]{1,0:T(8,128)(2,1)S(1)}, bf16[512,512]{1,0:T(8,128)(2,1)}, u32[]{:S(2)}) copy-start(bf16[512,512]{1,0:T(8,128)(2,1)} %constant.34.clone.short_h_far) | copy-start | bytes 1572868
  7.7 1.0 %copy-start.7 = (f32[3,64,512]{2,1,0:T(8,128)S(1)}, f32[3,64,512]{2,1,0:T(8,128)}, u32[]{:S(2)}) copy-start(f32[3,64,512]{2,1,0:T(8,128)} %incoming.1) | copy-start | bytes 1179652
  8.7 0.7 %copy-start.8 = (f32[8,512]{1,0:T(8,128)S(1)}, f32[8,512]{1,0:T(8,128)}, u32[]{:S(2)}) copy-start(f32[8,512]{1,0:T(8,128)} %constant.31.clone.north) | copy-start | bytes 49156
  9.4 0.7 %copy-start.9 = (bf16[64,128]{1,0:T(8,128)(2,1)S(1)}, bf16[64,128]{1,0:T(8,128)(2,1)}, u32[]{:S(2)}) copy-start(bf16[64,128]{1,0:T(8,128)(2,1)} %constant.30.clone.pairs) | copy-start | bytes 49156
  50.4 0.8 %copy-start.12 = (f32[64,128,1]{1,0,2:T(8,128)S(1)}, f32[64,128,1]{1,0,2:T(8,128)}, u32[]{:S(2)}) copy-start(f32[64,128,1]{1,0,2:T(8,128)} %constant.47) | copy-start | bytes 98308
  50.4 1.6 %copy-start.10 = (f32[512,1024,1]{1,0,2:T(8,128)S(1)}, f32[512,1024,1]{1,0,2:T(8,128)}, u32[]{:S(2)}) copy-start(f32[512,1024,1]{1,0,2:T(8,128)} %constant.48) | copy-start | bytes 6291460
  50.9 1.7 %copy-start.11 = (f32[3,128,1024]{2,1,0:T(8,128)S(1)}, f32[3,128,1024]{2,1,0:T(8,128)}, u32[]{:S(2)}) copy-start(f32[3,128,1024]{2,1,0:T(8,128)} %get-tuple-element.7) | copy-start | bytes 4718596

commit v5 on v4

--- a/solution.py
+++ b/solution.py
@@ -87,12 +87,11 @@
     return row if isinstance(row, int) else pl.multiple_of(row, 8)
 
 
-def heun(state, fine, now, first, exchange_rims):
-    rows = state.shape[1]
+def heun(fine, now, first, exchange_rims):
+    rows, width = fine.shape[1:]
     blocks = (rows + 2 * HALO) // 8
-    pad = jnp.zeros((HALO, state.shape[2]), jnp.float32)
+    pad = jnp.zeros((HALO, width), jnp.float32)
     for f in range(3):
-        now[f, 16 : 16 + rows] = state[f]
         for ref in (now, first):
             ref[f, 0:8] = pad
             ref[f, 24 + rows : 32 + rows] = pad
@@ -143,14 +142,14 @@
 
 
 def kernel(
-    size, slices, state, incoming, pairs, north,
+    size, slices, state, incoming_far, pairs_far, north_far,
     wide_h_far, wide_l_far, short_h_far, short_l_far, along_h, along_l, back_h, back_l,
     east_far, sine_far, versine_far, fine, out,
-    now, first, mine, theirs, gap, landed, acc, change, relayed, leaving, returned,
+    incoming, north, pairs, now, first, mine, theirs, gap, landed, acc, change, relayed, leaving, returned,
     east, sine, versine, wide_h, wide_l, short_h, short_l, ah, al, bh, bl,
     fetch, x_send, x_recv, y_send, y_recv, t_send, t_recv, rim_send, rim_recv,
 ):
-    fields, rows, nc = incoming.shape
+    fields, rows, nc = incoming_far.shape
     half = nc // 2
     count = half // size
     me, slot = lax.axis_index("space"), lax.axis_index("tm")
@@ -163,6 +162,9 @@
         pltpu.make_async_copy(source, target, fetch.at[n])
         for n, (source, target) in enumerate(
             (
+                (state, now.at[:, pl.ds(16, state.shape[1])]),
+                (incoming_far, incoming),
+                (pairs_far, pairs),
                 (wide_h_far, wide_h),
                 (wide_l_far, wide_l),
                 (short_h_far, short_h),
@@ -172,6 +174,7 @@
                 (east_far.at[share], east),
                 (sine_far.at[share], sine),
                 (versine_far.at[share], versine),
+                (north_far, north),
                 (back_h, bh),
                 (back_l, bl),
             )
@@ -239,11 +242,11 @@
         pl.semaphore_wait(barrier, len(peers) + 2)
         for copy in rims:
             copy.start()
-        for copy in fetches[:4]:
+        for copy in fetches[1:7]:
             copy.wait()
         fresh = jnp.concatenate([incoming[f] for f in range(fields)], 0)
         fresh = spectra_of(fresh, short_h[...], short_l[...])
-        drift = x_spectra(state) - jnp.where(slot == 0, fresh, 0.0)
+        drift = x_spectra(now.at[:, pl.ds(16, wide_rows)]) - jnp.where(slot == 0, fresh, 0.0)
         lay_out(-drift, put_gap)
         for copy in rims:
             copy.wait()
@@ -253,7 +256,8 @@
             for copy in copies:
                 copy.start()
 
-    heun(state, fine, now, first, exchange_rims)
+    fetches[0].wait()
+    heun(fine, now, first, exchange_rims)
     lay_out(x_spectra(fine), put_mine)
     ahead = to_next(mine, theirs, 0)
 
@@ -261,7 +265,7 @@
     def _():
         ahead.start()
 
-    for copy in fetches[4:]:
+    for copy in fetches[7:]:
         copy.wait()
 
     @pl.when(slot > 0)
@@ -348,21 +352,23 @@
     blocks = (size, fields * count, 2 * rows)
     whole = (fields * count, 2 * nc)
     padded = (fields, state.shape[1] + 4 * HALO, width)
-    shapes = [padded] * 2 + [blocks] * 4 + [whole] * 3 + [blocks] * 2 + [(count, nc)] * 3
+    shapes = [incoming.shape, north.shape] + [padded] * 2 + [blocks] * 4 + [whole] * 3 + [blocks] * 2 + [(count, nc)] * 3
+    buffers = [pltpu.VMEM(shape, jnp.float32) for shape in shapes]
+    buffers[2:2] = [pltpu.VMEM(operands[2].shape, jnp.bfloat16)]
     vmem = pl.BlockSpec(memory_space=pltpu.VMEM)
-    far = pl.BlockSpec(memory_space=pl.ANY)
+    far = pl.BlockSpec(memory_space=pltpu.HBM)
     fine, moved = pl.pallas_call(
         functools.partial(kernel, size, slices),
         out_shape=[jax.ShapeDtypeStruct(shape, jnp.float32) for shape in (state.shape, blocks)],
-        in_specs=[vmem] * len(operands) + [far] * (len(distant) + 3),
+        in_specs=[far] * (len(operands) + len(distant) + 3),
         out_specs=[vmem] * 2,
-        scratch_shapes=[pltpu.VMEM(shape, jnp.float32) for shape in shapes]
+        scratch_shapes=buffers
         + [pltpu.VMEM(table.shape, jnp.bfloat16) for table in distant]
-        + [pltpu.SemaphoreType.DMA((len(distant) + 3,))]
+        + [pltpu.SemaphoreType.DMA((len(operands) + len(distant) + 3,))]
         + [pltpu.SemaphoreType.DMA((size - 1,))] * 4
         + [pltpu.SemaphoreType.DMA((2,))] * 4,
         compiler_params=pltpu.CompilerParams(
-            collective_id=0, has_side_effects=True, vmem_limit_bytes=48 << 20
+            collective_id=0, has_side_effects=True, vmem_limit_bytes=(64 << 20) - (128 << 10)
         ),
         cost_estimate=pl.CostEstimate(
             flops=40 * fields * count * nc * nc, bytes_accessed=32 * nc * nc, transcendentals=0

time: 55.9 us -> 45.8 us (0.82)
  local copies, waits for them, and re-layouts: 11.7 us -> 2.49 us
    unnamed x26 -> x6, local copies, waits for them, and re-layouts: 11.1 us -> 0.79 us
    reshape x2, local copies, waits for them, and re-layouts: 0.56 us -> 1.7 us  [shards(): moved = moved.reshape(size, fields, count, 2, rows).transpose(1, 4, 3, 0, 2)]
where the time goes in v5:
time: 45.8 us; the launch traced here: 45.7 us
  Pallas kernels  39.9 us (87%)
  matrix products  3.24 us (7%)
  local copies, waits for them, and re-layouts  2.49 us (5%)
    pallas_call x1, Pallas kernels, shards(): pl.pallas_call(functools.partial(kernel, size, slices), out_shape=[jax.Sh...  39.9 us
    dot_general x1, matrix products, shards(): result = fine + matmul('fYk,kx->fYx', moved, inverse.reshape(nc, width))  2.72 us
    reshape x2, local copies, waits for them, and re-layouts, shards(): moved = moved.reshape(size, fields, count, 2, rows).transpose(1, 4, 3, 0, 2)  1.7 us

profile of v5, /device:TPU:1, one launch (start us, length us, event | category | flops | bytes accessed | tf_op | source)
XLA Modules:
  0.0 45.7 jit_solution(4782454377060831477)
XLA Ops:
  0.0 39.9 %shard_map.163 = (f32[3,128,1024]{2,1,0:T(8,128)}, f32[8,96,128]{2,1,0:T(8,128)}) custom-call(f32[3,128,1024]{2,1,0:T(8,128)} %bitcast.15, f32[3,64,512]{2,1,0:T(8,128)} %incoming_far.1, bf16[64,128]{1,0:T(8,128)(2,1)} %constant.30.clone.pairs_far, f32[8,512]{1,0:T(8,128)} %constant.31.clone.north_far, bf16[512,1024]{1,0:T(8,128)(2,1)} %constant.32.clone.wide_h_far, ...), custom_call_target="tpu_custom_call" | custom-call | flops 1006632960 | bytes 8388608 | tf_op jit(solution)/shard_map/pallas_call | solution.py:360
  39.9 0.0 copy-start.2
  39.9 0.0 copy-start
  39.9 1.6 %reshape.6 = f32[8,3,32,2,64]{4,3,2,1,0:T(2,128)S(1)} reshape(f32[8,96,128]{2,1,0:T(8,128)} %get-tuple-element.8) | data formatting | bytes 786432 | tf_op jit(solution)/shard_map/reshape | solution.py:378
  41.5 0.0 copy-start.1
  41.5 0.1 copy.18
  41.6 0.0 copy-done.2
  41.6 0.5 %convolution_bitcast_fusion = f32[3,128,512]{2,1,0:T(8,128)S(1)} fusion(f32[3,64,512]{1,2,0:T(8,128)S(1)} %bitcast.14, f32[64,128,1]{1,0,2:T(8,128)S(1)} %copy-done.2), kind=kOutput, calls=%fused_computation.1 | convolution fusion | flops 75497472 | bytes 1212416 | tf_op jit(solution)/shard_map/yY,fyk->fYk/dot_general | solution.py:383
  42.2 0.0 copy-done
  42.2 0.8 %copy-done.1 = f32[3,128,1024]{2,1,0:T(8,128)S(1)} copy-done((f32[3,128,1024]{2,1,0:T(8,128)S(1)}, f32[3,128,1024]{2,1,0:T(8,128)}, u32[]{:S(2)}) %copy-start.1) | copy-done | bytes 1572888
  43.0 2.7 %add_bitcast_fusion = f32[1,3,128,1024]{3,2,1,0:T(8,128)} fusion(f32[3,128,1024]{2,1,0:T(8,128)S(1)} %copy-done.1, f32[3,128,512]{2,1,0:T(8,128)S(1)} %convolution_bitcast_fusion, f32[512,1024,1]{1,0,2:T(8,128)S(1)} %copy-done), kind=kOutput, calls=%fused_computation | convolution fusion | flops 1208352768 | bytes 6029312 | tf_op jit(solution)/shard_map/fYk,kx->fYx/dot_general | solution.py:384
Async XLA Ops:
  39.9 1.8 %copy-start.2 = (f32[64,128,1]{1,0,2:T(8,128)S(1)}, f32[64,128,1]{1,0,2:T(8,128)}, u32[]{:S(2)}) copy-start(f32[64,128,1]{1,0,2:T(8,128)} %constant.47) | copy-start | bytes 98308
  39.9 2.3 %copy-start = (f32[512,1024,1]{1,0,2:T(8,128)S(1)}, f32[512,1024,1]{1,0,2:T(8,128)}, u32[]{:S(2)}) copy-start(f32[512,1024,1]{1,0,2:T(8,128)} %constant.48) | copy-start | bytes 6291460
  41.5 1.4 %copy-start.1 = (f32[3,128,1024]{2,1,0:T(8,128)S(1)}, f32[3,128,1024]{2,1,0:T(8,128)}, u32[]{:S(2)}) copy-start(f32[3,128,1024]{2,1,0:T(8,128)} %get-tuple-element.7) | copy-start | bytes 4718596
